TPU v7x, 32 devices: a whole 2x2x4 slice. The times are simulated.
32 devices in a mesh: space: 16 (over z, y, x), dp: 2 (over core).
Axes of the slice: x: 2, y: 2, z: 4, core: 2. Of those that a mesh axis runs over, the one named last changes fastest.
Arguments:
- features: bfloat16 [192, 8, 8, 512], P(('space', 'dp')), may hold values from -6 to 6
- grad_out: bfloat16 [192, 8, 8, 512], P(('space', 'dp')), may hold values from -6 to 6
- occupancy: int32 [192, 512], P(('space', 'dp')), may hold values 0 or 1
- weight: bfloat16 [3, 3, 3, 64, 64], replicated, may hold values from -0.15625 to 0.15625
- neighbours: int32 [192, 26], P(('space', 'dp')), may hold values from 0 to 14, as said below
- send_rows: int32 [32, 4, 2], P(('space', 'dp')), may hold values from 0 to 6, as said below
Outputs:
- output: bfloat16 [192, 8, 8, 512], P(('space', 'dp'))
- feature_grad: bfloat16 [192, 8, 8, 512], P(('space', 'dp'))
- weight_grad: float32 [3, 3, 3, 64, 64], replicated
Inputs may be any that keep to these rules, and one draw needn't show every extreme that they name: `neighbours`: A value below 6 names another block of the same device; 6 + k * 2 + j names slot j of list k of the device k sends from, that is the device 1 lower, 1 higher, 2 lower, 2 higher along space for k = 0, 1, 2, 3 (same dp index); 14 names no block. Every filled slot of a list sent to a device is named by some entry of that device, and no unfilled slot is named. `send_rows`: list k of a device holds the blocks it sends to the device 1 higher, 1 lower, 2 higher, 2 lower along space for k = 0, 1, 2, 3 (same dp index); 6 marks an unfilled slot, filled slots come first and name distinct blocks; lists to devices outside the axis are unfilled.
All inputs are finite; a program needn't handle non-finite values. No bound on the sum of `occupancy` on one device may be relied on, other than what follows from the above.
Results may differ from a plain program's by a relative error of at most 0.003.
Values may be sent and summed in bfloat16 or wider, within the bound.
A program may use at most 128 MiB of HBM per device.

v0:
```python
import math

import jax
import jax.numpy as jnp
from jax import lax
from jax.sharding import PartitionSpec as P

DISTANCES = (1, -1, 2, -2)
OFFSETS = [
    (step_x, step_y, step_z)
    for step_x in (-1, 0, 1)
    for step_y in (-1, 0, 1)
    for step_z in (-1, 0, 1)
    if (step_x, step_y, step_z) != (0, 0, 0)
]
REACH = {-1: (7, 8, 0, 1), 0: (0, 8, 1, 9), 1: (0, 1, 9, 10)}


def shifted(block, axis, distance):
    devices = range(lax.axis_size(axis))
    route = [(i - distance, i) for i in devices if i - distance in devices]
    return lax.ppermute(block, axis, route)


def matmul(left, right, left_dim, right_dim):
    dims = (((left_dim,), (right_dim,)), ((), ()))
    return lax.dot_general(left, right, dims, preferred_element_type=jnp.float32)


def expand_mask(occupancy, channels):
    block_count = occupancy.shape[0]
    return jnp.repeat(occupancy.reshape(block_count, 8, 8, 8), channels, axis=3)


def band_weights(weight):
    channels = weight.shape[-1]
    zero_block = jnp.zeros((3, 3, channels, channels), weight.dtype)
    stacked = []
    for tap_in in range(4):
        parts = [
            weight[:, :, tap_in - out_pos] if 0 <= tap_in - out_pos <= 2 else zero_block
            for out_pos in range(2)
        ]
        stacked.append(jnp.concatenate(parts, axis=3))
    return jnp.concatenate(stacked, axis=2)


def window_rows(slab, channels):
    block_count = slab.shape[0]
    stacked = jnp.stack(
        [
            slab[..., 2 * channels * pair_num : 2 * channels * pair_num + 4 * channels]
            for pair_num in range(4)
        ],
        axis=3,
    )
    return stacked.reshape(block_count * 256, 4 * channels)


def face_regions(table, channels):
    regions = []
    for step_x, step_y, step_z in OFFSETS:
        x_low, x_high = REACH[step_x][:2]
        y_low, y_high = REACH[step_y][:2]
        z_low, z_high = REACH[step_z][:2]
        regions.append(table[:, x_low:x_high, y_low:y_high, z_low * channels : z_high * channels])
    return regions


def assemble(regions, centre, index):
    pieces = {(0, 0, 0): centre}
    for slot_num, offset in enumerate(OFFSETS):
        pieces[offset] = jnp.take(regions[slot_num], index[:, slot_num], axis=0)
    planes = []
    for step_x in (-1, 0, 1):
        lines = []
        for step_y in (-1, 0, 1):
            lines.append(
                jnp.concatenate([pieces[step_x, step_y, step_z] for step_z in (-1, 0, 1)], axis=3)
            )
        planes.append(jnp.concatenate(lines, axis=2))
    return jnp.concatenate(planes, axis=1)


def local_passes(padded, live_float, grads, banded):
    channels = banded.shape[-1] // 2
    block_count = padded.shape[0]
    grad_rows = grads.reshape(block_count * 256, 2 * channels)
    total = jnp.zeros((block_count * 256, 2 * channels), jnp.float32)
    dpad = jnp.zeros((block_count, 10, 10, 10 * channels), jnp.float32)
    dband = {}
    for shift_x in range(3):
        for shift_y in range(3):
            rows = window_rows(padded[:, shift_x : shift_x + 8, shift_y : shift_y + 8], channels)
            total = total + matmul(rows, banded[shift_x, shift_y], 1, 0)
            dband[shift_x, shift_y] = matmul(rows, grad_rows, 0, 0)
            back = matmul(grad_rows, banded[shift_x, shift_y], 1, 1).reshape(
                block_count, 8, 8, 4, 4 * channels
            )
            for pair_num in range(4):
                dpad = dpad.at[
                    :,
                    shift_x : shift_x + 8,
                    shift_y : shift_y + 8,
                    2 * channels * pair_num : 2 * channels * pair_num + 4 * channels,
                ].add(back[:, :, :, pair_num])
    output = (total.reshape(block_count, 8, 8, 8 * channels) * live_float).astype(jnp.bfloat16)

    def tap(shift_x, shift_y, shift_z):
        full = dband[shift_x, shift_y]
        terms = [
            full[
                (out_pos + shift_z) * channels : (out_pos + shift_z + 1) * channels,
                out_pos * channels : (out_pos + 1) * channels,
            ]
            for out_pos in range(2)
        ]
        return terms[0] + terms[1]

    dweight = jnp.stack(
        [
            jnp.stack(
                [
                    jnp.stack([tap(shift_x, shift_y, shift_z) for shift_z in range(3)])
                    for shift_y in range(3)
                ]
            )
            for shift_x in range(3)
        ]
    )
    return (output, dpad, dweight)


def on_device(features, grad_out, occupancy, weight, neighbours, send_rows):
    channels = weight.shape[-1]
    block_count = features.shape[0]
    slot_count = send_rows.shape[2]
    live = expand_mask(occupancy, channels) == 1
    shown = jnp.where(live, features, jnp.zeros_like(features))
    masked_grad = jnp.where(live, grad_out, jnp.zeros_like(grad_out))
    live_float = live.astype(jnp.float32)
    banded = band_weights(weight)
    send_plan = send_rows[0]
    spare = jnp.zeros((1, 8, 8, 8 * channels), jnp.bfloat16)
    source = jnp.concatenate([shown, spare], axis=0)
    received = []
    for peer_num, distance in enumerate(DISTANCES):
        outgoing = jnp.take(source, send_plan[peer_num], axis=0)
        arrived = shifted(outgoing, "space", distance)
        received.append(arrived)
    table = jnp.concatenate([shown] + received + [spare], axis=0)
    padded = assemble(face_regions(table, channels), shown, neighbours)
    output, dpad, dweight = local_passes(padded, live_float, masked_grad, banded)
    weight_total = lax.psum(dweight, ("space", "dp"))
    returned = jnp.zeros((table.shape[0], 8, 8, 8 * channels), jnp.float32)
    for slot_num, offset in enumerate(OFFSETS):
        xn0, xn1, xp0, xp1 = REACH[offset[0]]
        yn0, yn1, yp0, yp1 = REACH[offset[1]]
        zn0, zn1, zp0, zp1 = REACH[offset[2]]
        returned = returned.at[
            neighbours[:, slot_num], xn0:xn1, yn0:yn1, zn0 * channels : zn1 * channels
        ].add(dpad[:, xp0:xp1, yp0:yp1, zp0 * channels : zp1 * channels])
    inner = dpad[:, 1:9, 1:9, channels : 9 * channels] + returned[:block_count]
    accum = jnp.concatenate([inner, jnp.zeros((1, 8, 8, 8 * channels), jnp.float32)], axis=0)
    for peer_num, distance in enumerate(DISTANCES):
        start_row = block_count + peer_num * slot_count
        back_rows = returned[start_row : start_row + slot_count]
        arrived = shifted(back_rows.astype(jnp.bfloat16), "space", -distance).astype(
            back_rows.dtype
        )
        accum = accum.at[send_plan[peer_num]].add(arrived)
    feature_grad = (accum[:block_count] * live_float).astype(jnp.bfloat16)
    scale = 1.0 / math.sqrt(lax.axis_size("space") * lax.axis_size("dp") * block_count * 512)
    return (output, feature_grad, weight_total * scale)


def solution(mesh):
    return jax.shard_map(
        on_device,
        mesh=mesh,
        in_specs=(
            P(("space", "dp"), None, None, None),
            P(("space", "dp"), None, None, None),
            P(("space", "dp"), None),
            P(),
            P(("space", "dp"), None),
            P(("space", "dp"), None, None),
        ),
        out_specs=(P(("space", "dp"), None, None, None), P(("space", "dp"), None, None, None), P()),
        check_vma=False,
    )
```

profile of v0, /device:TPU:0, one launch (start us, length us, event | category | flops | bytes accessed | tf_op | source)
XLA Modules:
  0.0 2189.9 jit_solution(16349793866871355475)
XLA Ops:
  285.5 71.5 %while.62 = (s32[]{:T(128)}, f32[15,8,8,512]{3,2,1,0:T(8,128)}, s32[6,4]{0,1:T(4,128)S(1)}, f32[6,1,1,64]{3,2,1,0:T(1,128)}, s32[]{:T(128)}, /*index=5*/s32[4]{0:T(128)S(1)}) while((s32[]{:T(128)}, f32[15,8,8,512]{3,2,1,0:T(8,128)}, s32[6,4]{0,1:T(4,128)S(1)}, f32[6,1,1,64]{3,2,1,0:T(1,128)}, s32[]{:T(128)}, /*index=5*/s32[4]{0:T(128)S(1)}) %tuple.815), condition=%wide.while_cond.36, body=%wide.while_body.36.sunk | while | flops 157 | bytes 1475 | solution.py:162
  357.7 58.4 %while.63 = (s32[]{:T(128)}, f32[15,8,8,512]{3,2,1,0:T(8,128)}, s32[6,3]{0,1:T(4,128)S(1)}, f32[6,1,1,512]{3,2,1,0:T(1,128)}, s32[]{:T(128)}, /*index=5*/s32[4]{0:T(128)S(1)}, s32[1]{0:T(128)}, s32[]{:T(128)}) while((s32[]{:T(128)}, f32[15,8,8,512]{3,2,1,0:T(8,128)}, s32[6,3]{0,1:T(4,128)S(1)}, f32[6,1,1,512]{3,2,1,0:T(1,128)}, s32[]{:T(128)}, ...), condition=%wide.while_cond.37, body=%wide.while_body.37.sunk | while | flops 1053 | bytes 10431 | solution.py:162
  416.0 69.6 %while.64 = (s32[]{:T(128)}, f32[15,8,8,512]{3,2,1,0:T(8,128)}, s32[6,4]{0,1:T(4,128)S(1)}, f32[6,1,1,64]{3,2,1,0:T(1,128)}, s32[]{:T(128)}, /*index=5*/s32[4]{0:T(128)S(1)}) while((s32[]{:T(128)}, f32[15,8,8,512]{3,2,1,0:T(8,128)}, s32[6,4]{0,1:T(4,128)S(1)}, f32[6,1,1,64]{3,2,1,0:T(1,128)}, s32[]{:T(128)}, /*index=5*/s32[4]{0:T(128)S(1)}) %tuple.816), condition=%wide.while_cond.38, body=%wide.while_body.38.sunk | while | flops 157 | bytes 1475 | solution.py:162
  490.5 58.4 %while.65 = (s32[]{:T(128)}, f32[15,8,8,512]{3,2,1,0:T(8,128)}, s32[6,3]{0,1:T(4,128)S(1)}, f32[6,1,8,64]{3,2,1,0:T(8,128)}, s32[]{:T(128)}, /*index=5*/s32[4]{0:T(128)S(1)}, s32[1]{0:T(128)}, s32[]{:T(128)}) while((s32[]{:T(128)}, f32[15,8,8,512]{3,2,1,0:T(8,128)}, s32[6,3]{0,1:T(4,128)S(1)}, f32[6,1,8,64]{3,2,1,0:T(8,128)}, s32[]{:T(128)}, ...), condition=%wide.while_cond.39, body=%wide.while_body.39.sunk | while | flops 1053 | bytes 10431 | solution.py:162
  590.8 59.6 %while.67 = (s32[]{:T(128)}, f32[15,8,8,512]{3,2,1,0:T(8,128)}, s32[6,3]{0,1:T(4,128)S(1)}, f32[6,1,8,64]{3,2,1,0:T(8,128)}, s32[]{:T(128)}, /*index=5*/s32[4]{0:T(128)S(1)}, s32[1]{0:T(128)}, s32[]{:T(128)}) while((s32[]{:T(128)}, f32[15,8,8,512]{3,2,1,0:T(8,128)}, s32[6,3]{0,1:T(4,128)S(1)}, f32[6,1,8,64]{3,2,1,0:T(8,128)}, s32[]{:T(128)}, ...), condition=%wide.while_cond.41, body=%wide.while_body.41.sunk | while | flops 1053 | bytes 10431 | solution.py:162
  650.4 68.5 %while.68 = (s32[]{:T(128)}, f32[15,8,8,512]{3,2,1,0:T(8,128)}, s32[6,4]{0,1:T(4,128)S(1)}, f32[6,1,1,64]{3,2,1,0:T(1,128)}, s32[]{:T(128)}, /*index=5*/s32[4]{0:T(128)S(1)}) while((s32[]{:T(128)}, f32[15,8,8,512]{3,2,1,0:T(8,128)}, s32[6,4]{0,1:T(4,128)S(1)}, f32[6,1,1,64]{3,2,1,0:T(1,128)}, s32[]{:T(128)}, /*index=5*/s32[4]{0:T(128)S(1)}) %tuple.817), condition=%wide.while_cond.42, body=%wide.while_body.42.sunk | while | flops 157 | bytes 1475 | solution.py:162
  718.9 57.6 %while.69 = (s32[]{:T(128)}, f32[15,8,8,512]{3,2,1,0:T(8,128)}, s32[6,3]{0,1:T(4,128)S(1)}, f32[6,1,1,512]{3,2,1,0:T(1,128)}, s32[]{:T(128)}, /*index=5*/s32[4]{0:T(128)S(1)}, s32[1]{0:T(128)}, s32[]{:T(128)}) while((s32[]{:T(128)}, f32[15,8,8,512]{3,2,1,0:T(8,128)}, s32[6,3]{0,1:T(4,128)S(1)}, f32[6,1,1,512]{3,2,1,0:T(1,128)}, s32[]{:T(128)}, ...), condition=%wide.while_cond.43, body=%wide.while_body.43.sunk | while | flops 1053 | bytes 10431 | solution.py:162
  779.7 73.7 %while.70 = (s32[]{:T(128)}, f32[15,8,8,512]{3,2,1,0:T(8,128)}, s32[6,4]{0,1:T(4,128)S(1)}, f32[6,1,1,64]{3,2,1,0:T(1,128)}, s32[]{:T(128)}, /*index=5*/s32[4]{0:T(128)S(1)}) while((s32[]{:T(128)}, f32[15,8,8,512]{3,2,1,0:T(8,128)}, s32[6,4]{0,1:T(4,128)S(1)}, f32[6,1,1,64]{3,2,1,0:T(1,128)}, s32[]{:T(128)}, /*index=5*/s32[4]{0:T(128)S(1)}) %tuple.818), condition=%wide.while_cond.44, body=%wide.while_body.44.sunk | while | flops 157 | bytes 1475 | solution.py:162
  853.4 64.4 %while.71 = (s32[]{:T(128)}, f32[15,8,8,512]{3,2,1,0:T(8,128)}, s32[6,3]{0,1:T(4,128)S(1)}, f32[6,8,1,64]{3,2,1,0:T(1,128)S(1)}, s32[]{:T(128)}, /*index=5*/s32[4]{0:T(128)S(1)}, s32[1]{0:T(128)}, s32[]{:T(128)}) while((s32[]{:T(128)}, f32[15,8,8,512]{3,2,1,0:T(8,128)}, s32[6,3]{0,1:T(4,128)S(1)}, f32[6,8,1,64]{3,2,1,0:T(1,128)S(1)}, s32[]{:T(128)}, ...), condition=%wide.while_cond.45, body=%wide.while_body.45.sunk | while | flops 1053 | bytes 10431 | solution.py:162
  918.4 55.6 %while.72 = (s32[]{:T(128)}, f32[15,8,8,512]{3,2,1,0:T(8,128)}, s32[6,2]{0,1:T(2,128)S(1)}, f32[6,8,1,512]{3,2,1,0:T(1,128)}, s32[]{:T(128)}, /*index=5*/s32[4]{0:T(128)}, s32[1]{0:T(128)}, s32[]{:T(128)}) while((s32[]{:T(128)}, f32[15,8,8,512]{3,2,1,0:T(8,128)}, s32[6,2]{0,1:T(2,128)S(1)}, f32[6,8,1,512]{3,2,1,0:T(1,128)}, s32[]{:T(128)}, ...), condition=%wide.while_cond.46, body=%wide.while_body.46.sunk | while | flops 8221 | bytes 82087 | solution.py:162
  974.0 67.2 %while.73 = (s32[]{:T(128)}, f32[15,8,8,512]{3,2,1,0:T(8,128)}, s32[6,3]{0,1:T(4,128)}, f32[6,8,1,64]{3,2,1,0:T(1,128)}, s32[]{:T(128)}, /*index=5*/s32[4]{0:T(128)S(1)}, s32[1]{0:T(128)}, s32[]{:T(128)}) while((s32[]{:T(128)}, f32[15,8,8,512]{3,2,1,0:T(8,128)}, s32[6,3]{0,1:T(4,128)}, f32[6,8,1,64]{3,2,1,0:T(1,128)}, s32[]{:T(128)}, ...), condition=%wide.while_cond.47, body=%wide.while_body.47.sunk | while | flops 1053 | bytes 10431 | solution.py:162
  1043.1 59.5 %while.74 = (s32[]{:T(128)}, f32[15,8,8,512]{3,2,1,0:T(8,128)}, s32[6,2]{0,1:T(2,128)}, f32[6,8,8,64]{3,2,1,0:T(8,128)}, s32[]{:T(128)}, /*index=5*/s32[4]{0:T(128)}, s32[1]{0:T(128)}, s32[]{:T(128)}) while((s32[]{:T(128)}, f32[15,8,8,512]{3,2,1,0:T(8,128)}, s32[6,2]{0,1:T(2,128)}, f32[6,8,8,64]{3,2,1,0:T(8,128)}, s32[]{:T(128)}, ...), condition=%wide.while_cond.48, body=%wide.while_body.48.sunk | while | flops 8221 | bytes 82087 | solution.py:162
  1103.8 58.7 %while.75 = (s32[]{:T(128)}, f32[15,8,8,512]{3,2,1,0:T(8,128)}, s32[6,2]{0,1:T(2,128)}, f32[6,8,8,64]{3,2,1,0:T(8,128)}, s32[]{:T(128)}, /*index=5*/s32[4]{0:T(128)}, s32[1]{0:T(128)}, s32[]{:T(128)}) while((s32[]{:T(128)}, f32[15,8,8,512]{3,2,1,0:T(8,128)}, s32[6,2]{0,1:T(2,128)}, f32[6,8,8,64]{3,2,1,0:T(8,128)}, s32[]{:T(128)}, ...), condition=%wide.while_cond.49, body=%wide.while_body.49.sunk | while | flops 8221 | bytes 82087 | solution.py:162
  1162.5 69.4 %while.76 = (s32[]{:T(128)}, f32[15,8,8,512]{3,2,1,0:T(8,128)}, s32[6,3]{0,1:T(4,128)}, f32[6,8,1,64]{3,2,1,0:T(1,128)}, s32[]{:T(128)}, /*index=5*/s32[4]{0:T(128)S(1)}, s32[1]{0:T(128)}, s32[]{:T(128)}) while((s32[]{:T(128)}, f32[15,8,8,512]{3,2,1,0:T(8,128)}, s32[6,3]{0,1:T(4,128)}, f32[6,8,1,64]{3,2,1,0:T(1,128)}, s32[]{:T(128)}, ...), condition=%wide.while_cond.50, body=%wide.while_body.50.sunk | while | flops 1053 | bytes 10431 | solution.py:162
  1288.0 62.8 %while.78 = (s32[]{:T(128)}, f32[15,8,8,512]{3,2,1,0:T(8,128)}, s32[6,3]{0,1:T(4,128)S(1)}, f32[6,8,1,64]{3,2,1,0:T(1,128)}, s32[]{:T(128)}, /*index=5*/s32[4]{0:T(128)S(1)}, s32[1]{0:T(128)}, s32[]{:T(128)}) while((s32[]{:T(128)}, f32[15,8,8,512]{3,2,1,0:T(8,128)}, s32[6,3]{0,1:T(4,128)S(1)}, f32[6,8,1,64]{3,2,1,0:T(1,128)}, s32[]{:T(128)}, ...), condition=%wide.while_cond.52, body=%wide.while_body.52.sunk | while | flops 1053 | bytes 10431 | solution.py:162
  1350.8 73.2 %while.79 = (s32[]{:T(128)}, f32[15,8,8,512]{3,2,1,0:T(8,128)}, s32[6,4]{0,1:T(4,128)S(1)}, f32[6,1,1,64]{3,2,1,0:T(1,128)}, s32[]{:T(128)}, /*index=5*/s32[4]{0:T(128)S(1)}) while((s32[]{:T(128)}, f32[15,8,8,512]{3,2,1,0:T(8,128)}, s32[6,4]{0,1:T(4,128)S(1)}, f32[6,1,1,64]{3,2,1,0:T(1,128)}, s32[]{:T(128)}, /*index=5*/s32[4]{0:T(128)S(1)}) %tuple.819), condition=%wide.while_cond.53, body=%wide.while_body.53.sunk | while | flops 157 | bytes 1475 | solution.py:162
  1424.0 63.1 %while.80 = (s32[]{:T(128)}, f32[15,8,8,512]{3,2,1,0:T(8,128)}, s32[6,3]{0,1:T(4,128)}, f32[6,1,1,512]{3,2,1,0:T(1,128)}, s32[]{:T(128)}, /*index=5*/s32[4]{0:T(128)S(1)}, s32[1]{0:T(128)}, s32[]{:T(128)}) while((s32[]{:T(128)}, f32[15,8,8,512]{3,2,1,0:T(8,128)}, s32[6,3]{0,1:T(4,128)}, f32[6,1,1,512]{3,2,1,0:T(1,128)}, s32[]{:T(128)}, ...), condition=%wide.while_cond.54, body=%wide.while_body.54.sunk | while | flops 1053 | bytes 10431 | solution.py:162
  1487.0 69.6 %while.81 = (s32[]{:T(128)}, f32[15,8,8,512]{3,2,1,0:T(8,128)}, s32[6,4]{0,1:T(4,128)S(1)}, f32[6,1,1,64]{3,2,1,0:T(1,128)}, s32[]{:T(128)}, /*index=5*/s32[4]{0:T(128)S(1)}) while((s32[]{:T(128)}, f32[15,8,8,512]{3,2,1,0:T(8,128)}, s32[6,4]{0,1:T(4,128)S(1)}, f32[6,1,1,64]{3,2,1,0:T(1,128)}, s32[]{:T(128)}, /*index=5*/s32[4]{0:T(128)S(1)}) %tuple.820), condition=%wide.while_cond.55, body=%wide.while_body.55.sunk | while | flops 157 | bytes 1475 | solution.py:162
  1556.6 62.6 %while.82 = (s32[]{:T(128)}, f32[15,8,8,512]{3,2,1,0:T(8,128)}, s32[6,3]{0,1:T(4,128)}, f32[6,1,8,64]{3,2,1,0:T(8,128)S(1)}, s32[]{:T(128)}, /*index=5*/s32[4]{0:T(128)S(1)}, s32[1]{0:T(128)}, s32[]{:T(128)}) while((s32[]{:T(128)}, f32[15,8,8,512]{3,2,1,0:T(8,128)}, s32[6,3]{0,1:T(4,128)}, f32[6,1,8,64]{3,2,1,0:T(8,128)S(1)}, s32[]{:T(128)}, ...), condition=%wide.while_cond.56, body=%wide.while_body.56.sunk | while | flops 1053 | bytes 10431 | solution.py:162
  1655.2 58.8 %while.84 = (s32[]{:T(128)}, f32[15,8,8,512]{3,2,1,0:T(8,128)}, s32[6,3]{0,1:T(4,128)S(1)}, f32[6,1,8,64]{3,2,1,0:T(8,128)S(1)}, s32[]{:T(128)}, /*index=5*/s32[4]{0:T(128)S(1)}, s32[1]{0:T(128)}, s32[]{:T(128)}) while((s32[]{:T(128)}, f32[15,8,8,512]{3,2,1,0:T(8,128)}, s32[6,3]{0,1:T(4,128)S(1)}, f32[6,1,8,64]{3,2,1,0:T(8,128)S(1)}, s32[]{:T(128)}, ...), condition=%wide.while_cond.58, body=%wide.while_body.58.sunk | while | flops 1053 | bytes 10431 | solution.py:162
  1714.0 69.1 %while.85 = (s32[]{:T(128)}, f32[15,8,8,512]{3,2,1,0:T(8,128)}, s32[6,4]{0,1:T(4,128)S(1)}, f32[6,1,1,64]{3,2,1,0:T(1,128)}, s32[]{:T(128)}, /*index=5*/s32[4]{0:T(128)S(1)}) while((s32[]{:T(128)}, f32[15,8,8,512]{3,2,1,0:T(8,128)}, s32[6,4]{0,1:T(4,128)S(1)}, f32[6,1,1,64]{3,2,1,0:T(1,128)}, s32[]{:T(128)}, /*index=5*/s32[4]{0:T(128)S(1)}) %tuple.821), condition=%wide.while_cond.59, body=%wide.while_body.59.sunk | while | flops 157 | bytes 1475 | solution.py:162
  1783.1 58.5 %while.86 = (s32[]{:T(128)}, f32[15,8,8,512]{3,2,1,0:T(8,128)}, s32[6,3]{0,1:T(4,128)S(1)}, f32[6,1,1,512]{3,2,1,0:T(1,128)}, s32[]{:T(128)}, /*index=5*/s32[4]{0:T(128)S(1)}, s32[1]{0:T(128)}, s32[]{:T(128)}) while((s32[]{:T(128)}, f32[15,8,8,512]{3,2,1,0:T(8,128)}, s32[6,3]{0,1:T(4,128)S(1)}, f32[6,1,1,512]{3,2,1,0:T(1,128)}, s32[]{:T(128)}, ...), condition=%wide.while_cond.60, body=%wide.while_body.60.sunk | while | flops 1053 | bytes 10431 | solution.py:162
  1841.6 69.8 %while.87 = (s32[]{:T(128)}, f32[15,8,8,512]{3,2,1,0:T(8,128)}, s32[6,4]{0,1:T(4,128)S(1)}, f32[6,1,1,64]{3,2,1,0:T(1,128)}, s32[]{:T(128)}, /*index=5*/s32[4]{0:T(128)S(1)}) while((s32[]{:T(128)}, f32[15,8,8,512]{3,2,1,0:T(8,128)}, s32[6,4]{0,1:T(4,128)S(1)}, f32[6,1,1,64]{3,2,1,0:T(1,128)}, s32[]{:T(128)}, /*index=5*/s32[4]{0:T(128)S(1)}) %tuple.822), condition=%wide.while_cond.61, body=%wide.while_body.61.sunk | while | flops 157 | bytes 1475 | solution.py:162
  2064.2 116.4 %all-reduce.17.cloned.1.call-done = f32[3,3,3,64,64]{4,3,2,1,0:T(8,128)} async-done(((f32[3,3,3,64,64]{4,3,2,1,0:T(8,128)}), f32[3,3,3,64,64]{4,3,2,1,0:T(8,128)}) %all-reduce.17.cloned.1.call-update) | async-done | bytes 442384 | tf_op jit(solution)/shard_map/psum | solution.py:154
  (1435 shorter events, 2182.9 us)
Async XLA Ops:
  7.2 2173.5 %all-reduce.17.cloned.1.call-start = ((), (), s32[]{:S(2)}) async-start(), calls=%async_computation | async-start | bytes 1769472 | tf_op jit(solution)/shard_map/psum | solution.py:154
  8.3 21.0 copy-start.117
  13.0 18.9 copy-start.18
  13.0 20.3 copy-start.28
  14.3 1927.0 %collective-permute-start = (bf16[2,8,8,512]{3,2,1,0:T(8,128)(2,1)}, bf16[2,8,8,512]{3,2,1,0:T(8,128)(2,1)}, u32[]{:S(2)}, u32[]{:S(2)}) collective-permute-start(bf16[2,8,8,512]{3,2,1,0:T(8,128)(2,1)} %broadcast_select_fusion.25), channel_id=1, source_target_pairs={{0,2},{2,4},{4,6},{6,8},{8,10},{10,12},{12,14},{14,16},{16,18},{18... | collective-permute-start | bytes 393224 | tf_op jit(solution)/shard_map/ppermute | solution.py:22
  21.1 1926.3 %collective-permute-start.1 = (bf16[2,8,8,512]{3,2,1,0:T(8,128)(2,1)}, bf16[2,8,8,512]{3,2,1,0:T(8,128)(2,1)}, u32[]{:S(2)}, u32[]{:S(2)}) collective-permute-start(bf16[2,8,8,512]{3,2,1,0:T(8,128)(2,1)} %broadcast_select_fusion.24), channel_id=1, source_target_pairs={{2,0},{4,2},{6,4},{8,6},{10,8},{12,10},{14,12},{16,14},{18,16},{20... | collective-permute-start | bytes 393224 | tf_op jit(solution)/shard_map/ppermute | solution.py:22
  23.8 1925.9 %collective-permute-start.2 = (bf16[2,8,8,512]{3,2,1,0:T(8,128)(2,1)}, bf16[2,8,8,512]{3,2,1,0:T(8,128)(2,1)}, u32[]{:S(2)}, u32[]{:S(2)}) collective-permute-start(bf16[2,8,8,512]{3,2,1,0:T(8,128)(2,1)} %broadcast_select_fusion.23), channel_id=1, source_target_pairs={{0,4},{2,6},{4,8},{6,10},{8,12},{10,14},{12,16},{14,18},{16,20},{1... | collective-permute-start | bytes 393224 | tf_op jit(solution)/shard_map/ppermute | solution.py:22
  30.6 1925.2 %collective-permute-start.3 = (bf16[2,8,8,512]{3,2,1,0:T(8,128)(2,1)}, bf16[2,8,8,512]{3,2,1,0:T(8,128)(2,1)}, u32[]{:S(2)}, u32[]{:S(2)}) collective-permute-start(bf16[2,8,8,512]{3,2,1,0:T(8,128)(2,1)} %broadcast_select_fusion.22), channel_id=1, source_target_pairs={{4,0},{6,2},{8,4},{10,6},{12,8},{14,10},{16,12},{18,14},{20,16},{2... | collective-permute-start | bytes 393224 | tf_op jit(solution)/shard_map/ppermute | solution.py:22
  245.6 39.9 %copy-start.19 = (s32[4]{0:T(128)S(1)}, s32[4]{0:T(128)}, u32[]{:S(2)}) copy-start(s32[4]{0:T(128)} %constant.2373) | copy-start | bytes 52
  246.4 111.3 %copy-start.29 = (s32[4]{0:T(128)S(1)}, s32[4]{0:T(128)}, u32[]{:S(2)}) copy-start(s32[4]{0:T(128)} %constant.2383) | copy-start | bytes 52
  248.4 242.1 %copy-start.30 = (s32[4]{0:T(128)S(1)}, s32[4]{0:T(128)}, u32[]{:S(2)}) copy-start(s32[4]{0:T(128)} %constant.2407) | copy-start | bytes 52
  249.2 300.9 %copy-start.52 = (s32[4]{0:T(128)S(1)}, s32[4]{0:T(128)}, u32[]{:S(2)}) copy-start(s32[4]{0:T(128)} %constant.2421) | copy-start | bytes 52
  265.5 17.8 copy-start.74
  265.6 17.7 copy-start.76
  285.5 567.9 %copy-start.31 = (s32[4]{0:T(128)S(1)}, s32[4]{0:T(128)}, u32[]{:S(2)}) copy-start(s32[4]{0:T(128)} %constant.2481) | copy-start | bytes 52
  1162.5 456.8 %copy-start.103 = (s32[6,1]{0,1:T(1,128)S(1)}, s32[6,1]{0,1:T(1,128)}, u32[]{:S(2)}) copy-start(s32[6,1]{0,1:T(1,128)} %get-tuple-element.1143) | copy-start | bytes 76
  1162.5 456.8 %copy-start.53 = (s32[4]{0:T(128)S(1)}, s32[4]{0:T(128)}, u32[]{:S(2)}) copy-start(s32[4]{0:T(128)} %constant.2421) | copy-start | bytes 52
  1231.9 551.1 %copy-start.104 = (s32[6,1]{0,1:T(1,128)S(1)}, s32[6,1]{0,1:T(1,128)}, u32[]{:S(2)}) copy-start(s32[6,1]{0,1:T(1,128)} %get-tuple-element.1140) | copy-start | bytes 76
  1914.1 142.4 %collective-permute-start.4 = (bf16[2,8,8,512]{3,2,1,0:T(8,128)(2,1)}, bf16[2,8,8,512]{3,2,1,0:T(8,128)(2,1)}, u32[]{:S(2)}, u32[]{:S(2)}) collective-permute-start(bf16[2,8,8,512]{3,2,1,0:T(8,128)(2,1)} %get-tuple-element.997), channel_id=1, source_target_pairs={{2,0},{4,2},{6,4},{8,6},{10,8},{12,10},{14,12},{16,14},{18,16},{20... | collective-permute-start | bytes 393224 | tf_op jit(solution)/shard_map/ppermute | solution.py:22
  1925.4 21.1 copy-start.17
  1941.3 116.9 %collective-permute-start.5 = (bf16[2,8,8,512]{3,2,1,0:T(8,128)(2,1)}, bf16[2,8,8,512]{3,2,1,0:T(8,128)(2,1)}, u32[]{:S(2)}, u32[]{:S(2)}) collective-permute-start(bf16[2,8,8,512]{3,2,1,0:T(8,128)(2,1)} %get-tuple-element.996), channel_id=1, source_target_pairs={{0,2},{2,4},{4,6},{6,8},{8,10},{10,12},{12,14},{14,16},{16,18},{18... | collective-permute-start | bytes 393224 | tf_op jit(solution)/shard_map/ppermute | solution.py:22
  1947.5 112.4 %collective-permute-start.6 = (bf16[2,8,8,512]{3,2,1,0:T(8,128)(2,1)}, bf16[2,8,8,512]{3,2,1,0:T(8,128)(2,1)}, u32[]{:S(2)}, u32[]{:S(2)}) collective-permute-start(bf16[2,8,8,512]{3,2,1,0:T(8,128)(2,1)} %get-tuple-element.995), channel_id=1, source_target_pairs={{4,0},{6,2},{8,4},{10,6},{12,8},{14,10},{16,12},{18,14},{20,16},{2... | collective-permute-start | bytes 393224 | tf_op jit(solution)/shard_map/ppermute | solution.py:22
  1949.7 111.8 %collective-permute-start.7 = (bf16[2,8,8,512]{3,2,1,0:T(8,128)(2,1)}, bf16[2,8,8,512]{3,2,1,0:T(8,128)(2,1)}, u32[]{:S(2)}, u32[]{:S(2)}) collective-permute-start(bf16[2,8,8,512]{3,2,1,0:T(8,128)(2,1)} %get-tuple-element.994), channel_id=1, source_target_pairs={{0,4},{2,6},{4,8},{6,10},{8,12},{10,14},{12,16},{14,18},{16,20},{1... | collective-permute-start | bytes 393224 | tf_op jit(solution)/shard_map/ppermute | solution.py:22
  2013.3 17.5 copy-start.91
  (114 other events, 619.3 us)
Sparse Core Ops, SparseCore 0:
  2050.2 130.4 all-reduce.16
where the time goes:
time: 2230 us; the launch traced here: 2190 us
  other arithmetic  1120 us (50%)
  local copies, waits for them, and re-layouts  885 us (40%)
  waiting for transfers between devices  116 us (5%)
  starting transfers between devices  26.6 us (1%)
  matrix products  26 us (1%)
    scatter-add x312, other arithmetic  978 us
    scatter-add x456, local copies, waits for them, and re-layouts  627 us
    scatter-add x25, local copies, waits for them, and re-layouts, local_passes(): dpad = dpad.at[:, shift_x:shift_x + 8, shift_y:shift_y + 8, 2 * channels...  148 us
    psum x1, waiting for transfers between devices, on_device(): weight_total = lax.psum(dweight, ('space', 'dp'))  116 us
  transfers between devices with their start and end apart: 9, of which 1 were waited for; matrix products, arithmetic and copies ran while one was open for 92% of the time, Pallas kernels for 0%

commit v1 on v0

v1 whole, which is shorter than its diff:
```python
import functools
import math

import jax
import jax.numpy as jnp
from jax import lax
from jax.experimental import pallas as pl
from jax.experimental.pallas import tpu as pltpu
from jax.sharding import PartitionSpec as P

DISTANCES = (1, -1, 2, -2)
OFFSETS = [
    (step_x, step_y, step_z)
    for step_x in (-1, 0, 1)
    for step_y in (-1, 0, 1)
    for step_z in (-1, 0, 1)
    if (step_x, step_y, step_z) != (0, 0, 0)
]
SLOT = {offset: num for num, offset in enumerate(OFFSETS)}
PLANES = {-1: (7, 8, 0, 1), 0: (0, 8, 1, 9), 1: (0, 1, 9, 10)}
F32, BF16 = jnp.float32, jnp.bfloat16
VMEM = pl.BlockSpec(memory_space=pltpu.VMEM)
SMEM = pl.BlockSpec(memory_space=pltpu.SMEM)
LIMIT = 56 * 1024 * 1024


def shifted(block, axis, distance):
    devices = range(lax.axis_size(axis))
    route = [(i - distance, i) for i in devices if i - distance in devices]
    return lax.ppermute(block, axis, route)


def band_weights(weight):
    channels = weight.shape[-1]
    zero_block = jnp.zeros((3, 3, channels, channels), weight.dtype)
    stacked = []
    for tap_in in range(4):
        parts = [
            weight[:, :, tap_in - out_pos] if 0 <= tap_in - out_pos <= 2 else zero_block
            for out_pos in range(2)
        ]
        stacked.append(jnp.concatenate(parts, axis=3))
    return jnp.stack(stacked, axis=2)


def live_mask(occ):
    spread = (
        lax.broadcasted_iota(jnp.int32, (8, 512), 1) // 64
        == lax.broadcasted_iota(jnp.int32, (8, 512), 0)
    ).astype(BF16)
    return jnp.dot(occ, spread, preferred_element_type=F32).reshape(8, 8, 512)


def mask_feats(mask, values):
    return jnp.where(mask > 0.5, values.astype(F32), 0.0)


def outgoing_kernel(feat, occ, send, out):
    nb, cap = feat.shape[0], send.shape[2]
    for k in range(4):
        for j in range(cap):
            row = jnp.minimum(send[0, k, j], nb - 1)
            out[k, j] = mask_feats(live_mask(occ[row]), feat[row]).astype(BF16)


def build_bands(band, bands):
    zero = jnp.zeros((64, 128), BF16)
    for a in range(3):
        for c in range(3):
            for k, r in enumerate((0, 1, 2, 3, 4, None, None, -1)):
                for j in range(2):
                    d = None if r is None else r - 2 * j
                    piece = zero if d is None or not -1 <= d <= 2 else band[a, c, d + 1]
                    bands[c, 64 * k : 64 * k + 64, 256 * a + 128 * j : 256 * a + 128 * j + 128] = piece


def pair_store(dst, lead, row0, tiles, lanes):
    for b in range(0, len(tiles), 2):
        both = jnp.concatenate([tiles[b], tiles[b + 1]], axis=0).astype(BF16)
        if lead is None:
            dst[row0 + 8 * b : row0 + 8 * b + 16, lanes] = both
        else:
            dst[lead, row0 + 8 * b : row0 + 8 * b + 16, lanes] = both


def fill_grads(nb, grad, mask, gz, gt):
    wide = 8 * nb
    for x in (0, 1, 10, 11):
        gz[x * wide : (x + 1) * wide] = jnp.zeros((wide, 512), BF16)
    for b in range(0, nb, 2):
        one = mask_feats(mask[b], grad[b])
        two = mask_feats(mask[b + 1], grad[b + 1])
        both = jnp.concatenate([one, two], axis=1).astype(BF16)
        for x in range(8):
            row = (x + 2) * wide + 8 * b
            gz[row : row + 16] = both[x]
    flat = gz[2 * wide : 10 * wide].astype(F32).T.astype(BF16)
    gt[:, : 8 * wide] = flat[:256]
    gt[:, 8 * wide :] = flat[256:]


def nt_dot(left, right):
    return lax.dot_general(left, right, (((1,), (1,)), ((), ())), preferred_element_type=F32)


def back_matmuls(nb, gz, bands, dp):
    wide = 8 * nb
    for c in range(3):
        parts = []
        for w in range(2):
            left = jnp.concatenate(
                [gz[wide * (2 - a) : wide * (12 - a), 256 * w : 256 * w + 256] for a in range(3)],
                axis=1,
            )
            parts.append(nt_dot(left, bands[c]).reshape(10, nb, 8, 512))
        one, two = parts
        dp[c, :, :, :, 0:128] = one[..., 0:128]
        dp[c, :, :, :, 128:256] = one[..., 128:256] + two[..., 384:512]
        dp[c, :, :, :, 256:384] = one[..., 256:384] + two[..., 0:128]
        dp[c, :, :, :, 384:512] = two[..., 128:256]
        dp[c, :, :, :, 512:640] = one[..., 384:512] + two[..., 256:384]


def scatter(nb, dp, nbr, acc):
    acc[...] = jnp.zeros(acc.shape, F32)
    for b in range(nb):
        for ox in (0, -1, 1):
            x0, x1, p0, p1 = PLANES[ox]
            n = p1 - p0
            row = lax.broadcasted_iota(jnp.int32, (n, 8, 640), 1)
            low = lax.broadcasted_iota(jnp.int32, (n, 8, 128), 2) < 64
            flat = (n * 8, 640)

            def turned(value, by):
                return pltpu.roll(value, by, 1)

            r0 = turned(dp[0, p0:p1, b], 7)
            r2 = turned(dp[2, p0:p1, b], 1)
            tiles = {
                0: dp[1, p0:p1, b] + jnp.where(row < 7, r0, 0.0) + jnp.where(row > 0, r2, 0.0),
                -1: jnp.where(row == 7, r0, 0.0),
                1: jnp.where(row == 0, r2, 0.0),
            }
            for oy in (0, -1, 1):
                tile = tiles[oy]
                t = b if (ox, oy) == (0, 0) else nbr[b, SLOT[ox, oy, 0]]
                acc[t, x0:x1] += tile[..., :512]
                halo = tile[..., 512:]
                acc[nbr[b, SLOT[ox, oy, 1]], x0:x1, :, 0:128] += jnp.where(low, halo, 0.0)
                acc[nbr[b, SLOT[ox, oy, -1]], x0:x1, :, 384:512] += jnp.where(low, 0.0, halo)


def fill_padded(nb, table, nbr, pad):
    row = lax.broadcasted_iota(jnp.int32, (8, 640), 0)
    low = lax.broadcasted_iota(jnp.int32, (8, 128), 1) < 64
    for xp in range(10):
        ox = -1 if xp == 0 else 1 if xp == 9 else 0
        xs = {-1: 7, 0: xp - 1, 1: 0}[ox]
        shifts = ([], [], [])
        for b in range(nb):

            def tile(oy):
                t = b if (ox, oy) == (0, 0) else nbr[b, SLOT[ox, oy, 0]]
                up = table[nbr[b, SLOT[ox, oy, 1]], xs, :, 0:128]
                down = table[nbr[b, SLOT[ox, oy, -1]], xs, :, 384:512]
                return jnp.concatenate([table[t, xs], jnp.where(low, up, down)], axis=1)

            here = tile(0)
            shifts[0].append(pltpu.roll(jnp.where(row == 7, tile(-1), here), 1, 0))
            shifts[1].append(here)
            shifts[2].append(pltpu.roll(jnp.where(row == 0, tile(1), here), 7, 0))
        for c in range(3):
            pair_store(pad, c, xp * 8 * nb, shifts[c], slice(None))


def windows(nb, pad, a, c):
    rows = slice(8 * nb * a, 8 * nb * (a + 8))
    one = jnp.concatenate([pad[c, rows, 0:384], pad[c, rows, 512:640]], axis=1)
    two = jnp.concatenate([pad[c, rows, 256:640], pad[c, rows, 128:256]], axis=1)
    return one, two


def weight_matmuls(nb, pad, gt, packed):
    low = lax.broadcasted_iota(jnp.int32, (64, 128), 1) < 64
    for a in range(3):
        for c in range(3):
            one, two = windows(nb, pad, a, c)
            full = jnp.dot(gt[...], jnp.concatenate([one, two], axis=0), preferred_element_type=F32)

            def part(i, t):
                return full[64 * i : 64 * i + 64, 128 * t : 128 * t + 128]

            x0 = part(0, 3) + part(2, 0)
            x2 = part(1, 1) + part(3, 2)
            s02 = part(0, 0) + part(2, 1)
            s13 = part(1, 0) + part(3, 1)
            packed[0, 3 * a + c] = jnp.where(low, s02, x0) + pltpu.roll(s13, 64, 1)
            packed[1, 3 * a + c] = s02 + pltpu.roll(x2, 64, 1)


def forward(nb, pad, bands, mask, out):
    totals = [None, None]
    for a in range(3):
        for c in range(3):
            for w, rows in enumerate(windows(nb, pad, a, c)):
                term = jnp.dot(rows, bands[c, :, 256 * a : 256 * a + 256], preferred_element_type=F32)
                totals[w] = term if totals[w] is None else totals[w] + term
    for w in range(2):
        total = totals[w].reshape(8, nb, 8, 256)
        lanes = slice(256 * w, 256 * w + 256)
        for b in range(nb):
            out[b, :, :, lanes] = (total[:, b] * mask[b, :, :, lanes]).astype(BF16)


def fill_mask(nb, occ, mask):
    for b in range(nb):
        mask[b] = live_mask(occ[b])


def local_kernel(
    feat, grad, occ, band, got0, got1, got2, got3, nbr, out, inner, back, packed,
    mask, bands, gz, gt, dp, acc, table, pad,
):
    nb = feat.shape[0]
    cap = got0.shape[0]
    fill_mask(nb, occ, mask)
    build_bands(band, bands)
    fill_grads(nb, grad, mask, gz, gt)
    back_matmuls(nb, gz, bands, dp)
    scatter(nb, dp, nbr, acc)
    inner[...] = acc[:nb]
    for k in range(4):
        for j in range(cap):
            back[k, j] = acc[nb + k * cap + j].astype(BF16)
    for b in range(nb):
        table[b] = mask_feats(mask[b], feat[b])
    for k, got in enumerate((got0, got1, got2, got3)):
        for j in range(cap):
            table[nb + k * cap + j] = got[j].astype(F32)
    table[nb + 4 * cap] = jnp.zeros((8, 8, 512), F32)
    fill_padded(nb, table, nbr, pad)
    weight_matmuls(nb, pad, gt, packed)
    forward(nb, pad, bands, mask, out)


def final_kernel(inner, occ, got0, got1, got2, got3, send, out):
    nb, cap = inner.shape[0], got0.shape[0]
    for b in range(nb):
        total = inner[b]
        for k, got in enumerate((got0, got1, got2, got3)):
            for j in range(cap):
                total = total + jnp.where(send[0, k, j] == b, got[j].astype(F32), 0.0)
        out[b] = (total * live_mask(occ[b])).astype(BF16)


def on_device(features, grad_out, occupancy, weight, neighbours, send_rows):
    nb, cap = features.shape[0], send_rows.shape[2]
    slots = nb + 4 * cap + 1
    wide = 8 * nb
    params = pltpu.CompilerParams(vmem_limit_bytes=LIMIT)
    occ = (occupancy == 1).astype(BF16).reshape(nb, 64, 8)
    band = band_weights(weight)
    block = (8, 8, 512)
    outgoing = pl.pallas_call(
        outgoing_kernel,
        out_shape=jax.ShapeDtypeStruct((4, cap) + block, BF16),
        in_specs=[VMEM, VMEM, SMEM],
        out_specs=VMEM,
        compiler_params=params,
    )(features, occ, send_rows)
    got = [shifted(outgoing[k], "space", d) for k, d in enumerate(DISTANCES)]
    out, inner, back, packed = pl.pallas_call(
        local_kernel,
        out_shape=(
            jax.ShapeDtypeStruct((nb,) + block, BF16),
            jax.ShapeDtypeStruct((nb,) + block, F32),
            jax.ShapeDtypeStruct((4, cap) + block, BF16),
            jax.ShapeDtypeStruct((2, 9, 64, 128), F32),
        ),
        in_specs=[VMEM] * 8 + [SMEM],
        out_specs=(VMEM,) * 4,
        scratch_shapes=[
            pltpu.VMEM((nb,) + block, F32),
            pltpu.VMEM((3, 512, 768), BF16),
            pltpu.VMEM((12 * wide, 512), BF16),
            pltpu.VMEM((256, 16 * wide), BF16),
            pltpu.VMEM((3, 10, nb, 8, 640), F32),
            pltpu.VMEM((slots,) + block, F32),
            pltpu.VMEM((slots,) + block, F32),
            pltpu.VMEM((3, 10 * wide, 640), BF16),
        ],
        compiler_params=params,
    )(features, grad_out, occ, band, *got, neighbours)
    arrived = [shifted(back[k], "space", -d) for k, d in enumerate(DISTANCES)]
    feature_grad = pl.pallas_call(
        final_kernel,
        out_shape=jax.ShapeDtypeStruct((nb,) + block, BF16),
        in_specs=[VMEM] * 6 + [SMEM],
        out_specs=VMEM,
        compiler_params=params,
    )(inner, occ, *arrived, send_rows)
    scale = 1.0 / math.sqrt(lax.axis_size("space") * lax.axis_size("dp") * nb * 512)
    total = lax.psum(packed, ("space", "dp"))
    turned = jnp.swapaxes(total, 2, 3) * scale
    taps = jnp.stack([turned[0, :, 64:], turned[0, :, :64], turned[1, :, 64:]], axis=1)
    return out, feature_grad, taps.reshape(weight.shape)


def solution(mesh):
    whole = ("space", "dp")
    return jax.shard_map(
        on_device,
        mesh=mesh,
        in_specs=(
            P(whole, None, None, None),
            P(whole, None, None, None),
            P(whole, None),
            P(),
            P(whole, None),
            P(whole, None, None),
        ),
        out_specs=(P(whole, None, None, None), P(whole, None, None, None), P()),
        check_vma=False,
    )
```

time: 2230 us -> 181 us (0.08); the launches traced: 2190 us -> 180 us
  other arithmetic: 1120 us -> 3.98 us
  local copies, waits for them, and re-layouts: 885 us -> 5.7 us
  matrix products: 26 us -> 0 us
    scatter-add x327 -> x0, other arithmetic: 986 us -> none
    scatter-add x481 -> x0, local copies, waits for them, and re-layouts: 776 us -> none
    add x25 -> x0, other arithmetic: 45.5 us -> none  [the longest x24 43.2 us: local_passes(): dpad = dpad.at[:, shift_x:shift_x + 8, shift_y:shift_y + 8, 2 * channels...]
    unnamed x297 -> x23, local copies, waits for them, and re-layouts: 35.3 us -> 2.98 us
    select_n x64 -> x0, other arithmetic: 27 us -> none  [the longest x13 14.7 us: on_device(): returned = returned.at[neighbours[:, slot_num], xn0:xn1, yn0:yn1, zn0 * c...]
    dot_general x27 -> x0, matrix products: 26 us -> none  [matmul(): lax.dot_general(left, right, dims, preferred_element_type=jnp.float32)]
    gather x30 -> x0, local copies, waits for them, and re-layouts: 24 us -> none  [the longest x26 21.7 us: assemble(): pieces[offset] = jnp.take(regions[slot_num], index[:, slot_num], axis=0)]
  transfers between devices with their start and end apart: 9 -> 9, of which waited for: 1 -> 4; matrix products, arithmetic and copies ran while one was open for 92% -> 1% of each run, Pallas kernels for 0% -> 2%
where the time goes in v1:
time: 181 us; the launch traced here: 180 us
  waiting for transfers between devices  116 us (64%)
  starting transfers between devices  25.5 us (14%)
  Pallas kernels  14.6 us (8%)
  between operations  14.2 us (8%)
  local copies, waits for them, and re-layouts  5.7 us (3%)
  other arithmetic  3.98 us (2%)
    psum x1, waiting for transfers between devices, on_device(): total = lax.psum(packed, ('space', 'dp'))  107 us
    ppermute x8, starting transfers between devices, shifted(): return lax.ppermute(block, axis, route)  25.5 us
    pallas_call x1, Pallas kernels, on_device(): pl.pallas_call(local_kernel, out_shape=(jax.ShapeDtypeStruct((nb,) + bloc...  9.67 us
    ppermute x8, waiting for transfers between devices, shifted(): return lax.ppermute(block, axis, route)  8.6 us
  transfers between devices with their start and end apart: 9, of which 4 were waited for; matrix products, arithmetic and copies ran while one was open for 1% of the time, Pallas kernels for 2%

profile of v1, /device:TPU:0, one launch (start us, length us, event | category | flops | bytes accessed | tf_op | source)
XLA Modules:
  0.0 180.1 jit_solution(17538495609792713981)
XLA Ops:
  7.2 0.7 compare_convert_fusion
  7.9 0.8 reshape.21.occ
  8.7 0.7 copy.26.send
  9.4 2.1 %shard_map.85 = bf16[4,2,8,8,512]{4,3,2,1,0:T(8,128)(2,1)} custom-call(bf16[6,8,8,512]{3,2,1,0:T(8,128)(2,1)} %feat.3, bf16[6,64,8]{2,1,0:T(8,128)(2,1)} %reshape.21.occ, s32[1,4,2]{2,1,0:T(4,128)} %copy.26.send), custom_call_target="tpu_custom_call" | custom-call | tf_op jit(solution)/shard_map/pallas_call | solution.py:264
  11.5 1.2 slice_bitcast_fusion.3
  12.7 4.8 %collective-permute-start = (bf16[2,8,8,512]{3,2,1,0:T(8,128)(2,1)S(1)}, bf16[2,8,8,512]{3,2,1,0:T(8,128)(2,1)S(1)}, u32[]{:S(2)}, u32[]{:S(2)}) collective-permute-start(bf16[2,8,8,512]{3,2,1,0:T(8,128)(2,1)S(1)} %get-tuple-element.21), channel_id=1, source_target_pairs={{0,2},{2,4},{4,6},{6,8},{8,10},{10,12},{12,14},{14,16},{16,18},{18... | collective-permute-start | bytes 393224 | tf_op jit(solution)/shard_map/ppermute | solution.py:30
  17.5 1.3 collective-permute-start.1
  18.8 5.5 %collective-permute-start.2 = (bf16[2,8,8,512]{3,2,1,0:T(8,128)(2,1)S(1)}, bf16[2,8,8,512]{3,2,1,0:T(8,128)(2,1)S(1)}, u32[]{:S(2)}, u32[]{:S(2)}) collective-permute-start(bf16[2,8,8,512]{3,2,1,0:T(8,128)(2,1)S(1)} %get-tuple-element.19), channel_id=1, source_target_pairs={{0,4},{2,6},{4,8},{6,10},{8,12},{10,14},{12,16},{14,18},{16,20},{1... | collective-permute-start | bytes 393224 | tf_op jit(solution)/shard_map/ppermute | solution.py:30
  24.3 1.3 collective-permute-start.3
  25.9 0.9 pad_maximum_fusion.1.band
  26.9 4.7 %collective-permute-done.3.got3 = bf16[2,8,8,512]{3,2,1,0:T(8,128)(2,1)S(1)} collective-permute-done((bf16[2,8,8,512]{3,2,1,0:T(8,128)(2,1)S(1)}, bf16[2,8,8,512]{3,2,1,0:T(8,128)(2,1)S(1)}, u32[]{:S(2)}, u32[]{:S(2)}) %collective-permute-start.3) | collective-permute-done | bytes 131104 | tf_op jit(solution)/shard_map/ppermute | solution.py:30
  31.6 0.6 copy-done.9
  32.2 9.7 %shard_map.86 = (bf16[6,8,8,512]{3,2,1,0:T(8,128)(2,1)}, f32[6,8,8,512]{3,2,1,0:T(8,128)}, bf16[4,2,8,8,512]{4,3,2,1,0:T(8,128)(2,1)}, f32[2,9,64,128]{3,2,1,0:T(8,128)}) custom-call(bf16[6,8,8,512]{3,2,1,0:T(8,128)(2,1)} %feat.3, bf16[6,8,8,512]{3,2,1,0:T(8,128)(2,1)} %grad.1, bf16[6,64,8]{2,1,0:T(8,128)(2,1)} %reshape.21.occ, ...), custom_call_target="tpu_custom_call" | custom-call | tf_op jit(solution)/shard_map/pallas_call | solution.py:272
  41.9 1.0 copy-done
  43.0 1.3 collective-permute-start.4
  44.3 4.6 %collective-permute-start.5 = (bf16[2,8,8,512]{3,2,1,0:T(8,128)(2,1)S(1)}, bf16[2,8,8,512]{3,2,1,0:T(8,128)(2,1)S(1)}, u32[]{:S(2)}, u32[]{:S(2)}) collective-permute-start(bf16[2,8,8,512]{3,2,1,0:T(8,128)(2,1)S(1)} %get-tuple-element.16), channel_id=1, source_target_pairs={{0,2},{2,4},{4,6},{6,8},{8,10},{10,12},{12,14},{14,16},{16,18},{18... | collective-permute-start | bytes 393224 | tf_op jit(solution)/shard_map/ppermute | solution.py:30
  48.9 1.3 collective-permute-start.6
  50.2 5.4 %collective-permute-start.7 = (bf16[2,8,8,512]{3,2,1,0:T(8,128)(2,1)S(1)}, bf16[2,8,8,512]{3,2,1,0:T(8,128)(2,1)S(1)}, u32[]{:S(2)}, u32[]{:S(2)}) collective-permute-start(bf16[2,8,8,512]{3,2,1,0:T(8,128)(2,1)S(1)} %get-tuple-element.14), channel_id=1, source_target_pairs={{0,4},{2,6},{4,8},{6,10},{8,12},{10,14},{12,16},{14,18},{16,20},{1... | collective-permute-start | bytes 393224 | tf_op jit(solution)/shard_map/ppermute | solution.py:30
  55.7 1.1 collective-permute-done.6.got2
  56.7 2.8 %collective-permute-done.7.got3 = bf16[2,8,8,512]{3,2,1,0:T(8,128)(2,1)S(1)} collective-permute-done((bf16[2,8,8,512]{3,2,1,0:T(8,128)(2,1)S(1)}, bf16[2,8,8,512]{3,2,1,0:T(8,128)(2,1)S(1)}, u32[]{:S(2)}, u32[]{:S(2)}) %collective-permute-start.7) | collective-permute-done | bytes 131104 | tf_op jit(solution)/shard_map/ppermute | solution.py:30
  60.2 2.8 %shard_map.87 = bf16[6,8,8,512]{3,2,1,0:T(8,128)(2,1)} custom-call(f32[6,8,8,512]{3,2,1,0:T(8,128)} %get-tuple-element.8.inner, bf16[6,64,8]{2,1,0:T(8,128)(2,1)} %reshape.21.occ, bf16[2,8,8,512]{3,2,1,0:T(8,128)(2,1)} %copy-done.2, bf16[2,8,8,512]{3,2,1,0:T(8,128)(2,1)} %copy-done.3, bf16[2,8,8,512]{3,2,1,0:T(8,128)(2,1)} %copy-done.4, ...), custom_call_target="tpu_custom_call" | custom-call | tf_op jit(solution)/shard_map/pallas_call | solution.py:295
  63.0 107.5 %all-reduce.4.cloned.1.call-done = f32[2,9,64,128]{3,2,1,0:T(8,128)} async-done(((f32[2,9,64,128]{3,2,1,0:T(8,128)}), f32[2,9,64,128]{3,2,1,0:T(8,128)}) %all-reduce.4.cloned.1.call-update) | async-done | bytes 589840 | tf_op jit(solution)/shard_map/psum | solution.py:303
  170.5 1.1 multiply_bitcast_fusion
  172.3 1.0 pad_maximum_fusion
  (34 shorter events, 1.7 us)
Async XLA Ops:
  7.2 163.3 %all-reduce.4.cloned.1.call-start = ((), (), s32[]{:S(2)}) async-start(), calls=%async_computation | async-start | bytes 1179648 | tf_op jit(solution)/shard_map/psum | solution.py:303
  7.9 0.8 copy-start.10
  11.5 14.1 %copy-start.1 = (bf16[3,3,3,64,64]{4,3,2,1,0:T(8,128)(2,1)S(1)}, bf16[3,3,3,64,64]{4,3,2,1,0:T(8,128)(2,1)}, u32[]{:S(2)}) copy-start(bf16[3,3,3,64,64]{4,3,2,1,0:T(8,128)(2,1)} %param.9) | copy-start | bytes 663556
  12.7 14.2 %collective-permute-start = (bf16[2,8,8,512]{3,2,1,0:T(8,128)(2,1)S(1)}, bf16[2,8,8,512]{3,2,1,0:T(8,128)(2,1)S(1)}, u32[]{:S(2)}, u32[]{:S(2)}) collective-permute-start(bf16[2,8,8,512]{3,2,1,0:T(8,128)(2,1)S(1)} %get-tuple-element.21), channel_id=1, source_target_pairs={{0,2},{2,4},{4,6},{6,8},{8,10},{10,12},{12,14},{14,16},{16,18},{18... | collective-permute-start | bytes 393224 | tf_op jit(solution)/shard_map/ppermute | solution.py:30
  17.5 9.3 %collective-permute-start.1 = (bf16[2,8,8,512]{3,2,1,0:T(8,128)(2,1)S(1)}, bf16[2,8,8,512]{3,2,1,0:T(8,128)(2,1)S(1)}, u32[]{:S(2)}, u32[]{:S(2)}) collective-permute-start(bf16[2,8,8,512]{3,2,1,0:T(8,128)(2,1)S(1)} %get-tuple-element.20), channel_id=1, source_target_pairs={{2,0},{4,2},{6,4},{8,6},{10,8},{12,10},{14,12},{16,14},{18,16},{20... | collective-permute-start | bytes 393224 | tf_op jit(solution)/shard_map/ppermute | solution.py:30
  18.8 8.0 %collective-permute-start.2 = (bf16[2,8,8,512]{3,2,1,0:T(8,128)(2,1)S(1)}, bf16[2,8,8,512]{3,2,1,0:T(8,128)(2,1)S(1)}, u32[]{:S(2)}, u32[]{:S(2)}) collective-permute-start(bf16[2,8,8,512]{3,2,1,0:T(8,128)(2,1)S(1)} %get-tuple-element.19), channel_id=1, source_target_pairs={{0,4},{2,6},{4,8},{6,10},{8,12},{10,14},{12,16},{14,18},{16,20},{1... | collective-permute-start | bytes 393224 | tf_op jit(solution)/shard_map/ppermute | solution.py:30
  24.3 7.3 %collective-permute-start.3 = (bf16[2,8,8,512]{3,2,1,0:T(8,128)(2,1)S(1)}, bf16[2,8,8,512]{3,2,1,0:T(8,128)(2,1)S(1)}, u32[]{:S(2)}, u32[]{:S(2)}) collective-permute-start(bf16[2,8,8,512]{3,2,1,0:T(8,128)(2,1)S(1)} %get-tuple-element.18), channel_id=1, source_target_pairs={{4,0},{6,2},{8,4},{10,6},{12,8},{14,10},{16,12},{18,14},{20,16},{2... | collective-permute-start | bytes 393224 | tf_op jit(solution)/shard_map/ppermute | solution.py:30
  26.8 4.7 %copy-start.6 = (bf16[2,8,8,512]{3,2,1,0:T(8,128)(2,1)}, bf16[2,8,8,512]{3,2,1,0:T(8,128)(2,1)S(1)}, u32[]{:S(2)}) copy-start(bf16[2,8,8,512]{3,2,1,0:T(8,128)(2,1)S(1)} %collective-permute-done.got0) | copy-start | bytes 393220
  26.8 4.7 %copy-start.7 = (bf16[2,8,8,512]{3,2,1,0:T(8,128)(2,1)}, bf16[2,8,8,512]{3,2,1,0:T(8,128)(2,1)S(1)}, u32[]{:S(2)}) copy-start(bf16[2,8,8,512]{3,2,1,0:T(8,128)(2,1)S(1)} %collective-permute-done.1.got1) | copy-start | bytes 393220
  26.9 4.7 %copy-start.8 = (bf16[2,8,8,512]{3,2,1,0:T(8,128)(2,1)}, bf16[2,8,8,512]{3,2,1,0:T(8,128)(2,1)S(1)}, u32[]{:S(2)}) copy-start(bf16[2,8,8,512]{3,2,1,0:T(8,128)(2,1)S(1)} %collective-permute-done.2.got2) | copy-start | bytes 393220
  31.6 0.7 copy-start.9
  41.9 1.0 copy-start
  43.0 12.6 %collective-permute-start.4 = (bf16[2,8,8,512]{3,2,1,0:T(8,128)(2,1)S(1)}, bf16[2,8,8,512]{3,2,1,0:T(8,128)(2,1)S(1)}, u32[]{:S(2)}, u32[]{:S(2)}) collective-permute-start(bf16[2,8,8,512]{3,2,1,0:T(8,128)(2,1)S(1)} %get-tuple-element.17), channel_id=1, source_target_pairs={{2,0},{4,2},{6,4},{8,6},{10,8},{12,10},{14,12},{16,14},{18,16},{20... | collective-permute-start | bytes 393224 | tf_op jit(solution)/shard_map/ppermute | solution.py:30
  44.3 11.3 %collective-permute-start.5 = (bf16[2,8,8,512]{3,2,1,0:T(8,128)(2,1)S(1)}, bf16[2,8,8,512]{3,2,1,0:T(8,128)(2,1)S(1)}, u32[]{:S(2)}, u32[]{:S(2)}) collective-permute-start(bf16[2,8,8,512]{3,2,1,0:T(8,128)(2,1)S(1)} %get-tuple-element.16), channel_id=1, source_target_pairs={{0,2},{2,4},{4,6},{6,8},{8,10},{10,12},{12,14},{14,16},{16,18},{18... | collective-permute-start | bytes 393224 | tf_op jit(solution)/shard_map/ppermute | solution.py:30
  48.9 7.9 %collective-permute-start.6 = (bf16[2,8,8,512]{3,2,1,0:T(8,128)(2,1)S(1)}, bf16[2,8,8,512]{3,2,1,0:T(8,128)(2,1)S(1)}, u32[]{:S(2)}, u32[]{:S(2)}) collective-permute-start(bf16[2,8,8,512]{3,2,1,0:T(8,128)(2,1)S(1)} %get-tuple-element.15), channel_id=1, source_target_pairs={{4,0},{6,2},{8,4},{10,6},{12,8},{14,10},{16,12},{18,14},{20,16},{2... | collective-permute-start | bytes 393224 | tf_op jit(solution)/shard_map/ppermute | solution.py:30
  50.2 9.4 %collective-permute-start.7 = (bf16[2,8,8,512]{3,2,1,0:T(8,128)(2,1)S(1)}, bf16[2,8,8,512]{3,2,1,0:T(8,128)(2,1)S(1)}, u32[]{:S(2)}, u32[]{:S(2)}) collective-permute-start(bf16[2,8,8,512]{3,2,1,0:T(8,128)(2,1)S(1)} %get-tuple-element.14), channel_id=1, source_target_pairs={{0,4},{2,6},{4,8},{6,10},{8,12},{10,14},{12,16},{14,18},{16,20},{1... | collective-permute-start | bytes 393224 | tf_op jit(solution)/shard_map/ppermute | solution.py:30
  55.6 3.9 %copy-start.2 = (bf16[2,8,8,512]{3,2,1,0:T(8,128)(2,1)}, bf16[2,8,8,512]{3,2,1,0:T(8,128)(2,1)S(1)}, u32[]{:S(2)}) copy-start(bf16[2,8,8,512]{3,2,1,0:T(8,128)(2,1)S(1)} %collective-permute-done.4.got0) | copy-start | bytes 393220
  55.7 3.9 %copy-start.3 = (bf16[2,8,8,512]{3,2,1,0:T(8,128)(2,1)}, bf16[2,8,8,512]{3,2,1,0:T(8,128)(2,1)S(1)}, u32[]{:S(2)}) copy-start(bf16[2,8,8,512]{3,2,1,0:T(8,128)(2,1)S(1)} %collective-permute-done.5.got1) | copy-start | bytes 393220
  56.7 2.8 %copy-start.4 = (bf16[2,8,8,512]{3,2,1,0:T(8,128)(2,1)}, bf16[2,8,8,512]{3,2,1,0:T(8,128)(2,1)S(1)}, u32[]{:S(2)}) copy-start(bf16[2,8,8,512]{3,2,1,0:T(8,128)(2,1)S(1)} %collective-permute-done.6.got2) | copy-start | bytes 393220
  59.5 0.6 copy-start.5
Sparse Core Ops, SparseCore 0:
  42.1 128.3 all-reduce.3

commit v2 on v1

--- a/solution.py
+++ b/solution.py
@@ -24,10 +24,25 @@
 LIMIT = 56 * 1024 * 1024
 
 
-def shifted(block, axis, distance):
-    devices = range(lax.axis_size(axis))
-    route = [(i - distance, i) for i in devices if i - distance in devices]
-    return lax.ppermute(block, axis, route)
+MESH = pl.DeviceIdType.MESH
+TILES = 14
+
+
+def greet(partners):
+    barrier = pltpu.get_barrier_semaphore()
+    for device in partners:
+        pl.semaphore_signal(barrier, inc=1, device_id=device, device_id_type=MESH)
+
+
+def greeted(count):
+    pl.semaphore_wait(pltpu.get_barrier_semaphore(), count)
+
+
+def remote(src, dst, send_sem, recv_sem, device):
+    return pltpu.make_async_remote_copy(
+        src_ref=src, dst_ref=dst, send_sem=send_sem, recv_sem=recv_sem,
+        device_id=device, device_id_type=MESH,
+    )
 
 
 def band_weights(weight):
@@ -55,12 +70,20 @@
     return jnp.where(mask > 0.5, values.astype(F32), 0.0)
 
 
-def outgoing_kernel(feat, occ, send, out):
+def lend_kernel(n, feat, occ, send, got, held, send_sem, recv_sem):
     nb, cap = feat.shape[0], send.shape[2]
+    here, core = lax.axis_index("space"), lax.axis_index("dp")
+    partners = [(lax.rem(here + d + n, n), core) for d in DISTANCES]
+    greet(partners)
     for k in range(4):
         for j in range(cap):
             row = jnp.minimum(send[0, k, j], nb - 1)
-            out[k, j] = mask_feats(live_mask(occ[row]), feat[row]).astype(BF16)
+            held[k, j] = mask_feats(live_mask(occ[row]), feat[row]).astype(BF16)
+        if k == 0:
+            greeted(4)
+        remote(held.at[k], got.at[k], send_sem.at[k], recv_sem.at[k], partners[k]).start()
+    for k in range(4):
+        remote(held.at[k], got.at[k], send_sem.at[k], recv_sem.at[k], partners[k]).wait()
 
 
 def build_bands(band, bands):
@@ -181,6 +204,7 @@
 
 
 def weight_matmuls(nb, pad, gt, packed):
+    odd = []
     low = lax.broadcasted_iota(jnp.int32, (64, 128), 1) < 64
     for a in range(3):
         for c in range(3):
@@ -194,8 +218,11 @@
             x2 = part(1, 1) + part(3, 2)
             s02 = part(0, 0) + part(2, 1)
             s13 = part(1, 0) + part(3, 1)
-            packed[0, 3 * a + c] = jnp.where(low, s02, x0) + pltpu.roll(s13, 64, 1)
-            packed[1, 3 * a + c] = s02 + pltpu.roll(x2, 64, 1)
+            packed[3 * a + c] = jnp.where(low, s02, x0) + pltpu.roll(s13, 64, 1)
+            odd.append(s02 + pltpu.roll(x2, 64, 1))
+    for q in range(5):
+        left = pltpu.roll(odd[min(2 * q + 1, 8)], 64, 1)
+        packed[9 + q] = jnp.where(low, left, odd[2 * q])
 
 
 def forward(nb, pad, bands, mask, out):
@@ -218,11 +245,11 @@
 
 
 def local_kernel(
-    feat, grad, occ, band, got0, got1, got2, got3, nbr, out, inner, back, packed,
+    feat, grad, occ, band, got, nbr, out, inner, back, packed,
     mask, bands, gz, gt, dp, acc, table, pad,
 ):
     nb = feat.shape[0]
-    cap = got0.shape[0]
+    cap = got.shape[1]
     fill_mask(nb, occ, mask)
     build_bands(band, bands)
     fill_grads(nb, grad, mask, gz, gt)
@@ -234,23 +261,106 @@
             back[k, j] = acc[nb + k * cap + j].astype(BF16)
     for b in range(nb):
         table[b] = mask_feats(mask[b], feat[b])
-    for k, got in enumerate((got0, got1, got2, got3)):
+    for k in range(4):
         for j in range(cap):
-            table[nb + k * cap + j] = got[j].astype(F32)
+            table[nb + k * cap + j] = got[k, j].astype(F32)
     table[nb + 4 * cap] = jnp.zeros((8, 8, 512), F32)
     fill_padded(nb, table, nbr, pad)
     weight_matmuls(nb, pad, gt, packed)
     forward(nb, pad, bands, mask, out)
 
 
-def final_kernel(inner, occ, got0, got1, got2, got3, send, out):
-    nb, cap = inner.shape[0], got0.shape[0]
+def final_kernel(
+    n, scale, inner, occ, back, packed, send, out, wout,
+    got, swapped, half, shards, full, other,
+    back_send, back_recv, rs_send, rs_recv, ag_send, ag_recv, core_send, core_recv,
+):
+    nb, cap = inner.shape[0], send.shape[2]
+    here, core = lax.axis_index("space"), lax.axis_index("dp")
+    twin = (here, 1 - core)
+    rows, shard = packed.shape[0] // 2, half.shape[1]
+    barrier = pltpu.get_barrier_semaphore()
+
+    def hello(k, _):
+        device = (lax.rem(here + k, n), core)
+        pl.semaphore_signal(barrier, inc=1, device_id=device, device_id_type=MESH)
+        return 0
+
+    lax.fori_loop(1, n, hello, 0)
+    pl.semaphore_signal(barrier, inc=1, device_id=twin, device_id_type=MESH)
+    pl.semaphore_wait(barrier, n)
+
+    theirs = pl.ds(pl.multiple_of((1 - core) * rows, 64), rows)
+    mine = pl.ds(pl.multiple_of(core * rows, 64), rows)
+    swap = remote(packed.at[theirs], swapped, core_send.at[0], core_recv.at[0], twin)
+    swap.start()
+    backs = [
+        remote(back.at[k], got.at[k], back_send.at[k], back_recv.at[k], (lax.rem(here - d + n, n), core))
+        for k, d in enumerate(DISTANCES)
+    ]
+    swap.wait()
+    summed = packed[mine] + swapped[...]
+    spare = n * shard - rows
+    if spare:
+        summed = jnp.concatenate([summed, jnp.zeros((spare, 128), F32)], axis=0)
+    half[...] = summed.reshape(n, shard, 128)
+
+    def reduce_copy(k):
+        to = lax.rem(here + k, n)
+        return remote(half.at[to], shards.at[k - 1], rs_send.at[k - 1], rs_recv.at[k - 1], (to, core))
+
+    def gather_copy(k):
+        to = lax.rem(here + k, n)
+        return remote(full.at[here], full.at[here], ag_send.at[k - 1], ag_recv.at[k - 1], (to, core))
+
+    def gather_arrival(k):
+        slot = lax.rem(here - k + n, n)
+        return remote(full.at[slot], full.at[slot], ag_send.at[k - 1], ag_recv.at[k - 1], (slot, core))
+
+    def each(action):
+        def body(k, _):
+            action(k)
+            return 0
+
+        lax.fori_loop(1, n, body, 0)
+
+    each(lambda k: reduce_copy(k).start())
+    for copy in backs:
+        copy.start()
+    each(lambda k: reduce_copy(k).wait())
+    total = half[here] + jnp.sum(shards[...], axis=0)
+    full[here] = (total * scale).astype(BF16)
+    each(lambda k: gather_copy(k).start())
+
+    for copy in backs:
+        copy.wait()
     for b in range(nb):
         total = inner[b]
-        for k, got in enumerate((got0, got1, got2, got3)):
+        for k in range(4):
             for j in range(cap):
-                total = total + jnp.where(send[0, k, j] == b, got[j].astype(F32), 0.0)
+                total = total + jnp.where(send[0, k, j] == b, got[k, j].astype(F32), 0.0)
         out[b] = (total * live_mask(occ[b])).astype(BF16)
+
+    each(lambda k: gather_copy(k).wait_send())
+    each(lambda k: gather_arrival(k).wait_recv())
+    swap = remote(full, other, core_send.at[1], core_recv.at[1], twin)
+    swap.start()
+    swap.wait()
+    own = full[...].astype(F32).reshape(n * shard, 128)[:rows]
+    far = other[...].astype(F32).reshape(n * shard, 128)[:rows]
+    low = jnp.where(core == 0, own, far)
+    high = jnp.where(core == 0, far, own)
+    every = jnp.concatenate([low, high], axis=0)
+    for q in range(TILES):
+        turned = every[64 * q : 64 * q + 64].T
+        if q < 9:
+            wout[3 * q + 1] = turned[:64]
+            wout[3 * q] = turned[64:]
+        else:
+            pair = 2 * (q - 9)
+            wout[3 * pair + 2] = turned[64:]
+            if pair + 1 < 9:
+                wout[3 * pair + 5] = turned[:64]
 
 
 def on_device(features, grad_out, occupancy, weight, neighbours, send_rows):
@@ -261,23 +371,30 @@
     occ = (occupancy == 1).astype(BF16).reshape(nb, 64, 8)
     band = band_weights(weight)
     block = (8, 8, 512)
-    outgoing = pl.pallas_call(
-        outgoing_kernel,
+    n = lax.axis_size("space")
+    got = pl.pallas_call(
+        functools.partial(lend_kernel, n),
         out_shape=jax.ShapeDtypeStruct((4, cap) + block, BF16),
         in_specs=[VMEM, VMEM, SMEM],
         out_specs=VMEM,
-        compiler_params=params,
+        scratch_shapes=[
+            pltpu.VMEM((4, cap) + block, BF16),
+            pltpu.SemaphoreType.DMA((4,)),
+            pltpu.SemaphoreType.DMA((4,)),
+        ],
+        compiler_params=pltpu.CompilerParams(
+            vmem_limit_bytes=LIMIT, collective_id=0, has_side_effects=True
+        ),
     )(features, occ, send_rows)
-    got = [shifted(outgoing[k], "space", d) for k, d in enumerate(DISTANCES)]
     out, inner, back, packed = pl.pallas_call(
         local_kernel,
         out_shape=(
             jax.ShapeDtypeStruct((nb,) + block, BF16),
             jax.ShapeDtypeStruct((nb,) + block, F32),
             jax.ShapeDtypeStruct((4, cap) + block, BF16),
-            jax.ShapeDtypeStruct((2, 9, 64, 128), F32),
+            jax.ShapeDtypeStruct((TILES, 64, 128), F32),
         ),
-        in_specs=[VMEM] * 8 + [SMEM],
+        in_specs=[VMEM] * 5 + [SMEM],
         out_specs=(VMEM,) * 4,
         scratch_shapes=[
             pltpu.VMEM((nb,) + block, F32),
@@ -290,20 +407,39 @@
             pltpu.VMEM((3, 10 * wide, 640), BF16),
         ],
         compiler_params=params,
-    )(features, grad_out, occ, band, *got, neighbours)
-    arrived = [shifted(back[k], "space", -d) for k, d in enumerate(DISTANCES)]
-    feature_grad = pl.pallas_call(
-        final_kernel,
-        out_shape=jax.ShapeDtypeStruct((nb,) + block, BF16),
-        in_specs=[VMEM] * 6 + [SMEM],
-        out_specs=VMEM,
-        compiler_params=params,
-    )(inner, occ, *arrived, send_rows)
-    scale = 1.0 / math.sqrt(lax.axis_size("space") * lax.axis_size("dp") * nb * 512)
-    total = lax.psum(packed, ("space", "dp"))
-    turned = jnp.swapaxes(total, 2, 3) * scale
-    taps = jnp.stack([turned[0, :, 64:], turned[0, :, :64], turned[1, :, 64:]], axis=1)
-    return out, feature_grad, taps.reshape(weight.shape)
+    )(features, grad_out, occ, band, got, neighbours)
+    scale = 1.0 / math.sqrt(n * lax.axis_size("dp") * nb * 512)
+    rows = TILES * 64 // 2
+    shard = -(-rows // (16 * n)) * 16
+    feature_grad, weight_grad = pl.pallas_call(
+        functools.partial(final_kernel, n, scale),
+        out_shape=(
+            jax.ShapeDtypeStruct((nb,) + block, BF16),
+            jax.ShapeDtypeStruct((27, 64, 64), F32),
+        ),
+        in_specs=[VMEM] * 4 + [SMEM],
+        out_specs=(VMEM, VMEM),
+        scratch_shapes=[
+            pltpu.VMEM((4, cap) + block, BF16),
+            pltpu.VMEM((rows, 128), F32),
+            pltpu.VMEM((n, shard, 128), F32),
+            pltpu.VMEM((n - 1, shard, 128), F32),
+            pltpu.VMEM((n, shard, 128), BF16),
+            pltpu.VMEM((n, shard, 128), BF16),
+            pltpu.SemaphoreType.DMA((4,)),
+            pltpu.SemaphoreType.DMA((4,)),
+            pltpu.SemaphoreType.DMA((n - 1,)),
+            pltpu.SemaphoreType.DMA((n - 1,)),
+            pltpu.SemaphoreType.DMA((n - 1,)),
+            pltpu.SemaphoreType.DMA((n - 1,)),
+            pltpu.SemaphoreType.DMA((2,)),
+            pltpu.SemaphoreType.DMA((2,)),
+        ],
+        compiler_params=pltpu.CompilerParams(
+            vmem_limit_bytes=LIMIT, collective_id=1, has_side_effects=True
+        ),
+    )(inner, occ, back, packed.reshape(2 * rows, 128), send_rows)
+    return out, feature_grad, weight_grad.reshape(weight.shape)
 
 
 def solution(mesh):

time: 181 us -> 67.4 us (0.37)
  waiting for transfers between devices: 116 us -> 0 us
  Pallas kernels: 14.6 us -> 57.4 us
  starting transfers between devices: 25.5 us -> 0 us
  between operations: 14.2 us -> 0.66 us
  other arithmetic: 3.98 us -> 1.88 us
    psum x1 -> x0, waiting for transfers between devices: 107 us -> none  [on_device(): total = lax.psum(packed, ('space', 'dp'))]
    pallas_call x2, Pallas kernels: 4.91 us -> 47.7 us  [the longest x1 30.6 us: on_device(): pl.pallas_call(functools.partial(final_kernel, n, scale), out_shape=(jax....]
    ppermute x8 -> x0, starting transfers between devices: 25.5 us -> none  [shifted(): return lax.ppermute(block, axis, route)]
    ppermute x8 -> x0, waiting for transfers between devices: 8.6 us -> none  [shifted(): return lax.ppermute(block, axis, route)]
    unnamed x23 -> x3, local copies, waits for them, and re-layouts: 2.98 us -> 5.27 us
  transfers between devices with their start and end apart: 9 -> 0, of which waited for: 4 -> 0; matrix products, arithmetic and copies ran while one was open for 1% -> 0% of each run, Pallas kernels for 2% -> 0%
where the time goes in v2:
time: 67.4 us; the launch traced here: 67 us
  Pallas kernels  57.4 us (85%)
  local copies, waits for them, and re-layouts  7.15 us (11%)
  other arithmetic  1.88 us (3%)
    pallas_call x1, Pallas kernels, on_device(): pl.pallas_call(functools.partial(final_kernel, n, scale), out_shape=(jax....  30.6 us
    pallas_call x1, Pallas kernels, on_device(): pl.pallas_call(functools.partial(lend_kernel, n), out_shape=jax.ShapeDtyp...  17 us
    pallas_call x1, Pallas kernels, on_device(): pl.pallas_call(local_kernel, out_shape=(jax.ShapeDtypeStruct((nb,) + bloc...  9.71 us
    unnamed x3, local copies, waits for them, and re-layouts  5.27 us

profile of v2, /device:TPU:0, one launch (start us, length us, event | category | flops | bytes accessed | tf_op | source)
XLA Modules:
  0.0 67.0 jit_solution(14151488710539189223)
XLA Ops:
  0.6 1.3 %copy.23.send = s32[1,4,2]{2,1,0:T(4,128)} copy(s32[1,4,2]{1,2,0:T(2,128)} %param.11) | data formatting | bytes 64 | tf_op args[5]
  2.0 0.7 %compare_convert_fusion = bf16[6,512]{1,0:T(8,128)(2,1)S(1)} fusion(s32[6,512]{1,0:T(8,128)} %param.8), kind=kLoop, calls=%fused_computation.8 | loop fusion | flops 6144 | bytes 18432 | tf_op jit(solution)/shard_map/reshape | solution.py:371
  2.7 0.8 %reshape.22.occ = bf16[6,64,8]{2,1,0:T(8,128)(2,1)} reshape(bf16[6,512]{1,0:T(8,128)(2,1)S(1)} %compare_convert_fusion) | data formatting | bytes 12288 | tf_op jit(solution)/shard_map/reshape | solution.py:371
  3.5 1.1 %slice_bitcast_fusion.2 = (bf16[3,3,64,64]{3,2,1,0:T(8,128)(2,1)S(1)}, bf16[3,3,64,64]{3,2,1,0:T(8,128)(2,1)S(1)}, bf16[3,3,64,64]{3,2,1,0:T(8,128)(2,1)S(1)}) fusion(bf16[3,3,3,64,64]{4,3,2,1,0:T(8,128)(2,1)} %param.9), kind=kLoop, calls=%fused_computation.7 | loop fusion | bytes 442368 | tf_op jit(solution)/shard_map/squeeze | solution.py:54
  4.6 0.3 pad_bitcast_fusion.1
  4.8 0.9 %pad_maximum_fusion.band = bf16[3,3,4,64,128]{4,3,2,1,0:T(8,128)(2,1)} fusion(bf16[3,3,1,64,128]{4,3,2,1,0:T(8,128)(2,1)S(1)} %get-tuple-element.21, bf16[3,3,1,64,128]{4,3,2,1,0:T(8,128)(2,1)S(1)} %get-tuple-element.20, bf16[3,3,1,64,128]{4,3,2,1,0:T(8,128)(2,1)S(1)} %get-tuple-element.19, bf16[3,3,1,64,128]{4,3,2,1,0:T(8,128)(2,1)S(1)} %get-tuple-element.18), kind=kLoop, calls=%fused_computation | loop fusion | flops 884736 | bytes 1179648 | tf_op jit(solution)/shard_map/stack | solution.py:58
  5.7 17.0 %shard_map.85.got = bf16[4,2,8,8,512]{4,3,2,1,0:T(8,128)(2,1)} custom-call(bf16[6,8,8,512]{3,2,1,0:T(8,128)(2,1)} %feat.3, bf16[6,64,8]{2,1,0:T(8,128)(2,1)} %reshape.22.occ, s32[1,4,2]{2,1,0:T(4,128)} %copy.23.send), custom_call_target="tpu_custom_call" | custom-call | tf_op jit(solution)/shard_map/pallas_call | solution.py:375
  22.8 9.7 %shard_map.86 = (bf16[6,8,8,512]{3,2,1,0:T(8,128)(2,1)}, f32[6,8,8,512]{3,2,1,0:T(8,128)}, bf16[4,2,8,8,512]{4,3,2,1,0:T(8,128)(2,1)}, f32[14,64,128]{2,1,0:T(8,128)}) custom-call(bf16[6,8,8,512]{3,2,1,0:T(8,128)(2,1)} %feat.3, bf16[6,8,8,512]{3,2,1,0:T(8,128)(2,1)} %grad.1, bf16[6,64,8]{2,1,0:T(8,128)(2,1)} %reshape.22.occ, ...), custom_call_target="tpu_custom_call" | custom-call | tf_op jit(solution)/shard_map/pallas_call | solution.py:389
  32.5 30.6 %shard_map.87 = (bf16[6,8,8,512]{3,2,1,0:T(8,128)(2,1)}, f32[27,64,64]{2,1,0:T(8,128)}) custom-call(f32[6,8,8,512]{3,2,1,0:T(8,128)} %get-tuple-element.10.inner, bf16[6,64,8]{2,1,0:T(8,128)(2,1)} %reshape.22.occ, bf16[4,2,8,8,512]{4,3,2,1,0:T(8,128)(2,1)} %get-tuple-element.11.back, f32[896,128]{1,0:T(8,128)} %bitcast.29, s32[1,4,2]{2,1,0:T(4,128)} %copy.23.send), custom_call_target="tpu_custom_call" | custom-call | tf_op jit(solution)/shard_map/pallas_call | solution.py:414
  63.1 1.8 %copy.30 = bf16[6,8,8,512]{3,2,1,0:T(8,128)(2,1)} copy(bf16[6,8,8,512]{3,2,1,0:T(8,128)(2,1)} %get-tuple-element.26) | data formatting | bytes 786432
  64.9 2.2 %copy.31 = f32[3,3,3,64,64]{4,3,2,1,0:T(8,128)} copy(f32[3,3,3,64,64]{4,3,2,1,0:T(8,128)} %bitcast.28) | data formatting | bytes 884736

commit v3 on v2

--- a/solution.py
+++ b/solution.py
@@ -28,16 +28,6 @@
 TILES = 14
 
 
-def greet(partners):
-    barrier = pltpu.get_barrier_semaphore()
-    for device in partners:
-        pl.semaphore_signal(barrier, inc=1, device_id=device, device_id_type=MESH)
-
-
-def greeted(count):
-    pl.semaphore_wait(pltpu.get_barrier_semaphore(), count)
-
-
 def remote(src, dst, send_sem, recv_sem, device):
     return pltpu.make_async_remote_copy(
         src_ref=src, dst_ref=dst, send_sem=send_sem, recv_sem=recv_sem,
@@ -45,55 +35,94 @@
     )
 
 
-def band_weights(weight):
-    channels = weight.shape[-1]
-    zero_block = jnp.zeros((3, 3, channels, channels), weight.dtype)
-    stacked = []
-    for tap_in in range(4):
-        parts = [
-            weight[:, :, tap_in - out_pos] if 0 <= tap_in - out_pos <= 2 else zero_block
-            for out_pos in range(2)
-        ]
-        stacked.append(jnp.concatenate(parts, axis=3))
-    return jnp.stack(stacked, axis=2)
-
-
-def live_mask(occ):
+def fill_mask(nb, occ, mask):
+    voxel = lax.broadcasted_iota(jnp.int32, (64, 512), 1) // 8
+    place = lax.broadcasted_iota(jnp.int32, (64, 512), 0)
     spread = (
-        lax.broadcasted_iota(jnp.int32, (8, 512), 1) // 64
-        == lax.broadcasted_iota(jnp.int32, (8, 512), 0)
-    ).astype(BF16)
-    return jnp.dot(occ, spread, preferred_element_type=F32).reshape(8, 8, 512)
+        lax.broadcasted_iota(jnp.int32, (512, 512), 0) % 8
+        == lax.broadcasted_iota(jnp.int32, (512, 512), 1) // 64
+    ).astype(F32).astype(BF16)
+    picks = [
+        jnp.where((voxel == place) & (occ[b : b + 1] == 1), 1.0, 0.0).astype(BF16) for b in range(nb)
+    ]
+    full = jnp.dot(jnp.concatenate(picks, axis=0), spread, preferred_element_type=F32)
+    mask[...] = full.reshape(nb, 8, 8, 512)
 
 
 def mask_feats(mask, values):
     return jnp.where(mask > 0.5, values.astype(F32), 0.0)
 
 
-def lend_kernel(n, feat, occ, send, got, held, send_sem, recv_sem):
-    nb, cap = feat.shape[0], send.shape[2]
+def inside(n, place):
+    return (place >= 0) & (place < n)
+
+
+def lend_kernel(n, feat, occ, send, got, held, mask, send_sem, recv_sem):
+    nb, cap = feat.shape[0], send.shape[0]
     here, core = lax.axis_index("space"), lax.axis_index("dp")
-    partners = [(lax.rem(here + d + n, n), core) for d in DISTANCES]
-    greet(partners)
+    barrier = pltpu.get_barrier_semaphore()
+    for d in DISTANCES:
+
+        @pl.when(inside(n, here + d))
+        def _():
+            pl.semaphore_signal(barrier, inc=1, device_id=(here + d, core), device_id_type=MESH)
+
+    fill_mask(nb, occ, mask)
     for k in range(4):
         for j in range(cap):
-            row = jnp.minimum(send[0, k, j], nb - 1)
-            held[k, j] = mask_feats(live_mask(occ[row]), feat[row]).astype(BF16)
-        if k == 0:
-            greeted(4)
-        remote(held.at[k], got.at[k], send_sem.at[k], recv_sem.at[k], partners[k]).start()
-    for k in range(4):
-        remote(held.at[k], got.at[k], send_sem.at[k], recv_sem.at[k], partners[k]).wait()
-
-
-def build_bands(band, bands):
+            row = jnp.minimum(send[j, k], nb - 1)
+            held[k, j] = mask_feats(mask[row], feat[row]).astype(BF16)
+    pl.semaphore_wait(barrier, sum(jnp.where(inside(n, here + d), 1, 0) for d in DISTANCES))
+    copies = exchange(n, here, core, held, got, send_sem, recv_sem, DISTANCES)
+    copies[0]()
+    copies[1]()
+
+
+def exchange(n, here, core, src, dst, send_sem, recv_sem, distances):
+    def copy(k):
+        return remote(
+            src.at[k], dst.at[k], send_sem.at[k], recv_sem.at[k], (here + distances[k], core)
+        )
+
+    def start():
+        for k, d in enumerate(distances):
+
+            @pl.when(inside(n, here + d))
+            def _():
+                copy(k).start()
+
+    def finish():
+        for k, d in enumerate(distances):
+
+            @pl.when(inside(n, here + d))
+            def _():
+                copy(k).wait_send()
+
+            @pl.when(inside(n, here - d))
+            def _():
+                copy(k).wait_recv()
+
+            @pl.when(jnp.logical_not(inside(n, here - d)))
+            def _():
+                dst[k] = jnp.zeros(dst.shape[1:], dst.dtype)
+
+    return start, finish
+
+
+def build_bands(weight, bands):
     zero = jnp.zeros((64, 128), BF16)
     for a in range(3):
         for c in range(3):
+            taps = [weight[9 * a + 3 * c + e] for e in range(3)]
+            none = jnp.zeros((64, 64), BF16)
+            pieces = [
+                jnp.concatenate(pair, axis=1)
+                for pair in zip(taps + [none], [none] + taps, strict=True)
+            ]
             for k, r in enumerate((0, 1, 2, 3, 4, None, None, -1)):
                 for j in range(2):
                     d = None if r is None else r - 2 * j
-                    piece = zero if d is None or not -1 <= d <= 2 else band[a, c, d + 1]
+                    piece = zero if d is None or not -1 <= d <= 2 else pieces[d + 1]
                     bands[c, 64 * k : 64 * k + 64, 256 * a + 128 * j : 256 * a + 128 * j + 128] = piece
 
 
@@ -239,19 +268,14 @@
             out[b, :, :, lanes] = (total[:, b] * mask[b, :, :, lanes]).astype(BF16)
 
 
-def fill_mask(nb, occ, mask):
-    for b in range(nb):
-        mask[b] = live_mask(occ[b])
-
-
 def local_kernel(
-    feat, grad, occ, band, got, nbr, out, inner, back, packed,
+    feat, grad, occ, weight, got, nbr, out, inner, back, packed,
     mask, bands, gz, gt, dp, acc, table, pad,
 ):
     nb = feat.shape[0]
     cap = got.shape[1]
     fill_mask(nb, occ, mask)
-    build_bands(band, bands)
+    build_bands(weight, bands)
     fill_grads(nb, grad, mask, gz, gt)
     back_matmuls(nb, gz, bands, dp)
     scatter(nb, dp, nbr, acc)
@@ -272,10 +296,10 @@
 
 def final_kernel(
     n, scale, inner, occ, back, packed, send, out, wout,
-    got, swapped, half, shards, full, other,
+    got, mask, swapped, half, shards, full, other,
     back_send, back_recv, rs_send, rs_recv, ag_send, ag_recv, core_send, core_recv,
 ):
-    nb, cap = inner.shape[0], send.shape[2]
+    nb, cap = inner.shape[0], send.shape[0]
     here, core = lax.axis_index("space"), lax.axis_index("dp")
     twin = (here, 1 - core)
     rows, shard = packed.shape[0] // 2, half.shape[1]
@@ -294,10 +318,9 @@
     mine = pl.ds(pl.multiple_of(core * rows, 64), rows)
     swap = remote(packed.at[theirs], swapped, core_send.at[0], core_recv.at[0], twin)
     swap.start()
-    backs = [
-        remote(back.at[k], got.at[k], back_send.at[k], back_recv.at[k], (lax.rem(here - d + n, n), core))
-        for k, d in enumerate(DISTANCES)
-    ]
+    start_backs, finish_backs = exchange(
+        n, here, core, back, got, back_send, back_recv, [-d for d in DISTANCES]
+    )
     swap.wait()
     summed = packed[mine] + swapped[...]
     spare = n * shard - rows
@@ -325,21 +348,20 @@
         lax.fori_loop(1, n, body, 0)
 
     each(lambda k: reduce_copy(k).start())
-    for copy in backs:
-        copy.start()
+    start_backs()
     each(lambda k: reduce_copy(k).wait())
     total = half[here] + jnp.sum(shards[...], axis=0)
     full[here] = (total * scale).astype(BF16)
     each(lambda k: gather_copy(k).start())
 
-    for copy in backs:
-        copy.wait()
+    fill_mask(nb, occ, mask)
+    finish_backs()
     for b in range(nb):
         total = inner[b]
         for k in range(4):
             for j in range(cap):
-                total = total + jnp.where(send[0, k, j] == b, got[k, j].astype(F32), 0.0)
-        out[b] = (total * live_mask(occ[b])).astype(BF16)
+                total = total + jnp.where(send[j, k] == b, got[k, j].astype(F32), 0.0)
+        out[b] = (total * mask[b]).astype(BF16)
 
     each(lambda k: gather_copy(k).wait_send())
     each(lambda k: gather_arrival(k).wait_recv())
@@ -368,8 +390,8 @@
     slots = nb + 4 * cap + 1
     wide = 8 * nb
     params = pltpu.CompilerParams(vmem_limit_bytes=LIMIT)
-    occ = (occupancy == 1).astype(BF16).reshape(nb, 64, 8)
-    band = band_weights(weight)
+    occ = occupancy
+    send_rows = send_rows.reshape(4, cap).T
     block = (8, 8, 512)
     n = lax.axis_size("space")
     got = pl.pallas_call(
@@ -379,6 +401,7 @@
         out_specs=VMEM,
         scratch_shapes=[
             pltpu.VMEM((4, cap) + block, BF16),
+            pltpu.VMEM((nb,) + block, F32),
             pltpu.SemaphoreType.DMA((4,)),
             pltpu.SemaphoreType.DMA((4,)),
         ],
@@ -407,7 +430,7 @@
             pltpu.VMEM((3, 10 * wide, 640), BF16),
         ],
         compiler_params=params,
-    )(features, grad_out, occ, band, got, neighbours)
+    )(features, grad_out, occ, weight.reshape(27, 64, 64), got, neighbours)
     scale = 1.0 / math.sqrt(n * lax.axis_size("dp") * nb * 512)
     rows = TILES * 64 // 2
     shard = -(-rows // (16 * n)) * 16
@@ -421,6 +444,7 @@
         out_specs=(VMEM, VMEM),
         scratch_shapes=[
             pltpu.VMEM((4, cap) + block, BF16),
+            pltpu.VMEM((nb,) + block, F32),
             pltpu.VMEM((rows, 128), F32),
             pltpu.VMEM((n, shard, 128), F32),
             pltpu.VMEM((n - 1, shard, 128), F32),

time: 67.4 us -> 55.6 us (0.82)
  Pallas kernels: 57.4 us -> 50.7 us
  local copies, waits for them, and re-layouts: 7.15 us -> 3.95 us
  other arithmetic: 1.88 us -> 0 us
    pallas_call x1, Pallas kernels: 17 us -> 13.2 us  [on_device(): pl.pallas_call(functools.partial(lend_kernel, n), out_shape=jax.ShapeDtyp...]
    pallas_call x1, Pallas kernels: 30.6 us -> 27.6 us  [on_device(): pl.pallas_call(functools.partial(final_kernel, n, scale), out_shape=(jax....]
    unnamed x3 -> x2, local copies, waits for them, and re-layouts: 5.27 us -> 3.95 us
    another operation x2 -> x0, other arithmetic: 1.16 us -> none  [band_weights(): return jnp.stack(stacked, axis=2)]
    squeeze x1 -> x0, local copies, waits for them, and re-layouts: 1.08 us -> none  [band_weights(): weight[:, :, tap_in - out_pos]]
    reshape x1 -> x0, local copies, waits for them, and re-layouts: 0.79 us -> none  [on_device(): occ = (occupancy == 1).astype(BF16).reshape(nb, 64, 8)]
    reshape x1 -> x0, other arithmetic: 0.72 us -> none  [on_device(): occ = (occupancy == 1).astype(BF16).reshape(nb, 64, 8)]
where the time goes in v3:
time: 55.6 us; the launch traced here: 55.3 us
  Pallas kernels  50.7 us (91%)
  local copies, waits for them, and re-layouts  3.95 us (7%)
  between operations  0.65 us (1%)
    pallas_call x1, Pallas kernels, on_device(): pl.pallas_call(functools.partial(final_kernel, n, scale), out_shape=(jax....  27.6 us
    pallas_call x1, Pallas kernels, on_device(): pl.pallas_call(functools.partial(lend_kernel, n), out_shape=jax.ShapeDtyp...  13.2 us
    pallas_call x1, Pallas kernels, on_device(): pl.pallas_call(local_kernel, out_shape=(jax.ShapeDtypeStruct((nb,) + bloc...  9.89 us
    unnamed x2, local copies, waits for them, and re-layouts  3.95 us

profile of v3, /device:TPU:0, one launch (start us, length us, event | category | flops | bytes accessed | tf_op | source)
XLA Modules:
  0.0 55.3 jit_solution(2261389178929503517)
XLA Ops:
  0.6 13.2 %shard_map.85.got = bf16[4,2,8,8,512]{4,3,2,1,0:T(8,128)(2,1)} custom-call(bf16[6,8,8,512]{3,2,1,0:T(8,128)(2,1)} %feat.3, s32[6,512]{1,0:T(8,128)} %occ.5, s32[2,4]{1,0:T(2,128)} %bitcast.9), custom_call_target="tpu_custom_call" | custom-call | tf_op jit(solution)/shard_map/pallas_call | solution.py:397
  13.9 9.9 %shard_map.86 = (bf16[6,8,8,512]{3,2,1,0:T(8,128)(2,1)}, f32[6,8,8,512]{3,2,1,0:T(8,128)}, bf16[4,2,8,8,512]{4,3,2,1,0:T(8,128)(2,1)}, f32[14,64,128]{2,1,0:T(8,128)}) custom-call(bf16[6,8,8,512]{3,2,1,0:T(8,128)(2,1)} %feat.3, bf16[6,8,8,512]{3,2,1,0:T(8,128)(2,1)} %grad.1, s32[6,512]{1,0:T(8,128)} %occ.5, bf16[27,64,64]{2,1,0:T(8,128)(2,1)} %bitcast.8, ...), custom_call_target="tpu_custom_call" | custom-call | tf_op jit(solution)/shard_map/pallas_call | solution.py:412
  23.8 27.6 %shard_map.87 = (bf16[6,8,8,512]{3,2,1,0:T(8,128)(2,1)}, f32[27,64,64]{2,1,0:T(8,128)}) custom-call(f32[6,8,8,512]{3,2,1,0:T(8,128)} %get-tuple-element.10.inner, s32[6,512]{1,0:T(8,128)} %occ.5, bf16[4,2,8,8,512]{4,3,2,1,0:T(8,128)(2,1)} %get-tuple-element.11.back, f32[896,128]{1,0:T(8,128)} %bitcast.7, s32[2,4]{1,0:T(2,128)} %bitcast.10), custom_call_target="tpu_custom_call" | custom-call | tf_op jit(solution)/shard_map/pallas_call | solution.py:437
  51.3 1.8 %copy.11 = bf16[6,8,8,512]{3,2,1,0:T(8,128)(2,1)} copy(bf16[6,8,8,512]{3,2,1,0:T(8,128)(2,1)} %get-tuple-element.19) | data formatting | bytes 786432
  53.1 2.2 %copy.12 = f32[3,3,3,64,64]{4,3,2,1,0:T(8,128)} copy(f32[3,3,3,64,64]{4,3,2,1,0:T(8,128)} %bitcast.6) | data formatting | bytes 884736
